TPU v7x, 32 devices: a whole 2x2x4 slice. The times are simulated.
32 devices in a mesh: blk: 8 (over z, y), rep: 4 (over x, core).
Axes of the slice: x: 2, y: 2, z: 4, core: 2. Of those that a mesh axis runs over, the one named last changes fastest.
Arguments:
- features: bfloat16 [8192, 256], P(('blk', 'rep')), may hold values from -6 to 6
- w_self: bfloat16 [256, 256], replicated, may hold values from -0.375 to 0.375
- w_neigh: bfloat16 [256, 256], replicated, may hold values from -0.375 to 0.375
- bias: float32 [256], replicated, may hold values from -3 to 3
- cotangent: bfloat16 [8192, 256], P(('blk', 'rep')), may hold values from -6 to 6
- tile_values: bfloat16 [8, 4, 8, 12, 128, 128], P('blk', 'rep')
- tile_rows: int32 [8, 4, 8, 12], P('blk', 'rep'), may hold values from 0 to 7, as said below
- tile_cols: int32 [8, 4, 8, 12], P('blk', 'rep'), may hold values from 0 to 1
- tile_counts: int32 [8, 4, 8], P('blk', 'rep'), may hold values from 1 to 12, as said below
Outputs:
- output: bfloat16 [8192, 256], P(('blk', 'rep'))
- grad_features: bfloat16 [8192, 256], P(('blk', 'rep'))
- grad_self: float32 [256, 256], replicated
- grad_neigh: float32 [256, 256], replicated
- grad_bias: float32 [256], replicated
Inputs may be any that keep to these rules, and one draw needn't show every extreme that they name: Among the live slots s < tile_counts[b, r, c] of one b, r, c, the pairs (tile_rows, tile_cols) are distinct; slots from tile_counts[b, r, c] on are not part of the adjacency. `tile_counts`: some entry equals 12 in every draw.
All inputs are finite; a program needn't handle non-finite values.
Results may differ from a plain program's by a relative error of at most 0.02.
Values may be sent and summed in bfloat16 or wider, within the bound.
A program may use at most 64 MiB of HBM per device.

v0:
```python
import jax
import jax.numpy as jnp
from jax import lax
from jax.sharding import PartitionSpec as P


def dense_layer(x_rows, agg_rows, cot_rows, w_self, w_neigh, bias):
    zvals = (
        jnp.dot(x_rows, w_self, preferred_element_type=jnp.float32)
        + jnp.dot(agg_rows, w_neigh, preferred_element_type=jnp.float32)
        + bias
    )
    sig = jax.nn.sigmoid(zvals)
    output = (zvals * sig).astype(jnp.bfloat16)
    grad_z = (cot_rows.astype(jnp.float32) * sig * (1.0 + zvals * (1.0 - sig))).astype(jnp.bfloat16)
    grad_agg = jnp.einsum("ng,fg->nf", grad_z, w_neigh, preferred_element_type=jnp.float32).astype(
        jnp.bfloat16
    )
    return (output, grad_z, grad_agg)


def local(
    features, w_self, w_neigh, bias, cotangent, tile_values, tile_rows, tile_cols, tile_counts
):
    rows_dev = features.shape[0]
    width = features.shape[1]
    values = tile_values[0, 0]
    row_ids = tile_rows[0, 0]
    col_ids = tile_cols[0, 0]
    counts = tile_counts[0, 0]
    slots = values.shape[1]
    tile = values.shape[2]
    per_dev = rows_dev // tile
    nblk = lax.axis_size("blk")
    nrep = lax.axis_size("rep")
    alive_all = lax.broadcasted_iota(jnp.int32, (nblk, slots), 1) < counts[:, None]

    def slot_data(block):
        vals = lax.dynamic_index_in_dim(values, block, 0, keepdims=False)
        rows_here = lax.dynamic_index_in_dim(row_ids, block, 0, keepdims=False)
        cols_here = lax.dynamic_index_in_dim(col_ids, block, 0, keepdims=False)
        alive = lax.dynamic_index_in_dim(alive_all, block, 0, keepdims=False)
        return (vals, rows_here, cols_here, alive)

    empty = jnp.zeros((nrep * per_dev, tile, width), jnp.float32)
    piece = lax.all_gather(features, "blk", axis=0, tiled=True)
    tiles = piece.reshape(piece.shape[0] // tile, tile, width)

    def add_one_block(j, acc):
        vals, rows_here, cols_here, alive = slot_data(j)
        picked = jnp.take(tiles, j * per_dev + cols_here, axis=0)
        prod = jnp.einsum("sij,sjf->sif", vals, picked, preferred_element_type=jnp.float32)
        prod = jnp.where(alive[:, None, None], prod, 0.0)
        return acc.at[rows_here].add(prod)

    partial_value = lax.fori_loop(0, piece.shape[0] // rows_dev, add_one_block, empty)
    partial_value = partial_value.reshape(nrep * rows_dev, width)
    agg_sum = lax.psum_scatter(
        partial_value.astype(jnp.bfloat16), "rep", scatter_dimension=0, tiled=True
    )
    output, grad_z, grad_agg = dense_layer(features, agg_sum, cotangent, w_self, w_neigh, bias)
    grad_agg_full = lax.all_gather(grad_agg, "rep", axis=0, tiled=True)
    grad_tiles = grad_agg_full.reshape(nrep * per_dev, tile, width)
    grad_self, grad_neigh, grad_bias = lax.psum(
        (
            jnp.einsum("nf,ng->fg", features, grad_z, preferred_element_type=jnp.float32),
            jnp.einsum("nf,ng->fg", agg_sum, grad_z, preferred_element_type=jnp.float32),
            jnp.sum(grad_z.astype(jnp.float32), axis=0),
        ),
        ("blk", "rep"),
    )
    nblocks = rows_dev * lax.axis_size("blk") // rows_dev

    def column_one_block(j, acc):
        vals, rows_here, cols_here, alive = slot_data(j)
        picked = jnp.take(grad_tiles, rows_here, axis=0)
        term = jnp.einsum("sji,sjf->sif", vals, picked, preferred_element_type=jnp.float32)
        term = jnp.where(alive[:, None, None], term, 0.0)
        return acc.at[j * per_dev + cols_here].add(term)

    start_acc = jnp.zeros((nblocks * per_dev, tile, width), jnp.float32)
    spread = lax.psum_scatter(
        lax.fori_loop(0, nblocks, column_one_block, start_acc)
        .reshape(rows_dev * lax.axis_size("blk"), width)
        .astype(jnp.bfloat16),
        "blk",
        scatter_dimension=0,
        tiled=True,
    ).astype(jnp.float32)
    own = jnp.einsum("ng,fg->nf", grad_z, w_self, preferred_element_type=jnp.float32)
    grad_features = (own + spread).astype(jnp.bfloat16)
    return (output, grad_features, grad_self, grad_neigh, grad_bias)


def solution(mesh):
    in_specs = (
        P(("blk", "rep"), None),
        P(),
        P(),
        P(),
        P(("blk", "rep"), None),
        P("blk", "rep", None, None, None, None),
        P("blk", "rep", None, None),
        P("blk", "rep", None, None),
        P("blk", "rep", None),
    )
    out_specs = (P(("blk", "rep"), None), P(("blk", "rep"), None), P(), P(), P())
    return jax.shard_map(local, mesh=mesh, in_specs=in_specs, out_specs=out_specs, check_vma=False)
```

profile of v0, /device:TPU:0, one launch (start us, length us, event | category | flops | bytes accessed | tf_op | source)
XLA Modules:
  0.0 342.4 jit_solution(11929674041958388004)
XLA Ops:
  8.7 44.3 %all-gather.2.cloned.1.call-done = bf16[2048,256]{1,0:T(8,128)(2,1)} async-done(((bf16[256,256]{1,0:T(8,128)(2,1)}), bf16[2048,256]{1,0:T(8,128)(2,1)}) %all-gather.2.cloned.1.call-update) | async-done | bytes 1048592 | tf_op jit(solution)/shard_map/all_gather | solution.py:46
  53.1 52.6 %while.26 = (s32[]{:T(128)}, f32[8,128,256]{2,1,0:T(8,128)S(1)}, s32[8,12]{1,0:T(8,128)}, pred[8,12]{1,0:T(8,128)(4,1)S(1)}, bf16[8,12,128,128]{3,2,1,0:T(8,128)...) while((s32[]{:T(128)}, f32[8,128,256]{2,1,0:T(8,128)S(1)}, ...), condition=%wide.region_2.3_spmd, body=%wide.region_0.2_spmd.sunk | while | flops 101844136 | bytes 9048645 | solution.py:56
  57.8 1.8 scatter_fusion
  64.4 1.8 scatter_fusion
  84.1 1.8 scatter_fusion
  97.3 1.8 scatter_fusion
  103.9 1.8 scatter_fusion
  106.7 4.7 %copy.14 = bf16[1,1,8,12,128,128]{4,5,3,2,1,0:T(8,128)(2,1)} copy(bf16[1,1,8,12,128,128]{5,4,3,2,1,0:T(8,128)(2,1)} %bitcast.84) | data formatting | bytes 6291456 | tf_op args[5]
  111.6 15.5 %reduce-scatter.3.cloned.1.call-done = bf16[256,256]{1,0:T(8,128)(2,1)} async-done(((bf16[1024,256]{1,0:T(8,128)(2,1)}), bf16[256,256]{1,0:T(8,128)(2,1)}) %reduce-scatter.3.cloned.1.call-update) | async-done | bytes 131088 | tf_op jit(solution)/shard_map/reduce_scatter | solution.py:58
  127.1 1.9 convert_reduce_fusion
  130.2 6.8 %all_gather.7 = bf16[1024,256]{1,0:T(8,128)(2,1)S(1)} all-gather(bf16[256,256]{1,0:T(8,128)(2,1)S(1)} %convolution_convert_fusion), channel_id=1, replica_groups=mesh['blk'=8,'rep'=4] {'rep'}, dimensions={0}, use_global_device_ids=true | all-gather | bytes 655360 | tf_op jit(solution)/shard_map/all_gather | solution.py:62
  139.6 62.1 %while.27 = (s32[]{:T(128)}, f32[16,128,256]{2,1,0:T(8,128)}, s32[8,12]{1,0:T(8,128)}, pred[8,12]{1,0:T(8,128)(4,1)S(1)}, bf16[8,12,128,128]{2,3,1,0:T(8,128)(2,...) while((s32[]{:T(128)}, f32[16,128,256]{2,1,0:T(8,128)}, ...), condition=%wide.region_6.7_spmd, body=%wide.region_4.6_spmd.sunk | while | flops 101844128 | bytes 9048641 | solution.py:83
  143.0 4.3 %scatter_fusion.1 = f32[16,128,256]{2,1,0:T(8,128)} fusion(f32[16,128,256]{2,1,0:T(8,128)} %get-tuple-element.435, s32[12]{0:T(128)S(1)} %get-tuple-element.396, f32[12,128,256]{2,1,0:T(8,128)S(1)} %convolution_select_fusion.5), kind=kCustom, calls=%fused_computation.3.clone.1 | custom fusion | flops 393216 | bytes 4718640 | tf_op jit(solution)/shard_map/while/body/eval_jaxpr/scatter-add | solution.py:79
  150.8 4.5 %scatter_fusion.1 = f32[16,128,256]{2,1,0:T(8,128)} fusion(f32[16,128,256]{2,1,0:T(8,128)} %get-tuple-element.435, s32[12]{0:T(128)S(1)} %get-tuple-element.396, f32[12,128,256]{2,1,0:T(8,128)S(1)} %convolution_select_fusion.5), kind=kCustom, calls=%fused_computation.3.clone.1 | custom fusion | flops 393216 | bytes 4718640 | tf_op jit(solution)/shard_map/while/body/eval_jaxpr/scatter-add | solution.py:79
  158.8 4.1 %scatter_fusion.1 = f32[16,128,256]{2,1,0:T(8,128)} fusion(f32[16,128,256]{2,1,0:T(8,128)} %get-tuple-element.435, s32[12]{0:T(128)S(1)} %get-tuple-element.396, f32[12,128,256]{2,1,0:T(8,128)S(1)} %convolution_select_fusion.5), kind=kCustom, calls=%fused_computation.3.clone.1 | custom fusion | flops 393216 | bytes 4718640 | tf_op jit(solution)/shard_map/while/body/eval_jaxpr/scatter-add | solution.py:79
  166.4 4.4 %scatter_fusion.1 = f32[16,128,256]{2,1,0:T(8,128)} fusion(f32[16,128,256]{2,1,0:T(8,128)} %get-tuple-element.435, s32[12]{0:T(128)S(1)} %get-tuple-element.396, f32[12,128,256]{2,1,0:T(8,128)S(1)} %convolution_select_fusion.5), kind=kCustom, calls=%fused_computation.3.clone.1 | custom fusion | flops 393216 | bytes 4718640 | tf_op jit(solution)/shard_map/while/body/eval_jaxpr/scatter-add | solution.py:79
  174.3 4.1 %scatter_fusion.1 = f32[16,128,256]{2,1,0:T(8,128)} fusion(f32[16,128,256]{2,1,0:T(8,128)} %get-tuple-element.435, s32[12]{0:T(128)S(1)} %get-tuple-element.396, f32[12,128,256]{2,1,0:T(8,128)S(1)} %convolution_select_fusion.5), kind=kCustom, calls=%fused_computation.3.clone.1 | custom fusion | flops 393216 | bytes 4718640 | tf_op jit(solution)/shard_map/while/body/eval_jaxpr/scatter-add | solution.py:79
  181.9 4.2 %scatter_fusion.1 = f32[16,128,256]{2,1,0:T(8,128)} fusion(f32[16,128,256]{2,1,0:T(8,128)} %get-tuple-element.435, s32[12]{0:T(128)S(1)} %get-tuple-element.396, f32[12,128,256]{2,1,0:T(8,128)S(1)} %convolution_select_fusion.5), kind=kCustom, calls=%fused_computation.3.clone.1 | custom fusion | flops 393216 | bytes 4718640 | tf_op jit(solution)/shard_map/while/body/eval_jaxpr/scatter-add | solution.py:79
  189.6 4.3 %scatter_fusion.1 = f32[16,128,256]{2,1,0:T(8,128)} fusion(f32[16,128,256]{2,1,0:T(8,128)} %get-tuple-element.435, s32[12]{0:T(128)S(1)} %get-tuple-element.396, f32[12,128,256]{2,1,0:T(8,128)S(1)} %convolution_select_fusion.5), kind=kCustom, calls=%fused_computation.3.clone.1 | custom fusion | flops 393216 | bytes 4718640 | tf_op jit(solution)/shard_map/while/body/eval_jaxpr/scatter-add | solution.py:79
  197.3 4.4 %scatter_fusion.1 = f32[16,128,256]{2,1,0:T(8,128)} fusion(f32[16,128,256]{2,1,0:T(8,128)} %get-tuple-element.435, s32[12]{0:T(128)S(1)} %get-tuple-element.396, f32[12,128,256]{2,1,0:T(8,128)S(1)} %convolution_select_fusion.5), kind=kCustom, calls=%fused_computation.3.clone.1 | custom fusion | flops 393216 | bytes 4718640 | tf_op jit(solution)/shard_map/while/body/eval_jaxpr/scatter-add | solution.py:79
  201.7 2.7 convert_element_type.39
  204.4 39.8 %psum.23 = f32[256]{0:T(256)} all-reduce(f32[256]{0:T(256)S(1)} %get-tuple-element.297), channel_id=1, replica_groups=mesh['blk'=8,'rep'=4] {'blk','rep'}, use_global_device_ids=true, to_apply=%region_11.12 | all-reduce | flops 256 | bytes 2048 | tf_op jit(solution)/shard_map/psum | solution.py:64
  244.2 22.4 %all-reduce.3.cloned.1.call-done = (f32[256,256]{0,1:T(8,128)}, f32[256,256]{1,0:T(8,128)}) async-done(((f32[256,256]{0,1:T(8,128)}, f32[256,256]{1,0:T(8,128)}), (f32[256,256]{0,1:T(8,128)}, f32[256,256]{1,0:T(8,128)})) %all-reduce.3.cloned.1.call-update) | async-done | bytes 524304 | tf_op jit(solution)/shard_map/psum | solution.py:64
  268.4 64.0 %reduce-scatter.5.cloned.1.call-done = bf16[256,256]{1,0:T(8,128)(2,1)} async-done(((bf16[2048,256]{1,0:T(8,128)(2,1)}), bf16[256,256]{1,0:T(8,128)(2,1)}) %reduce-scatter.5.cloned.1.call-update) | async-done | bytes 131088 | tf_op jit(solution)/shard_map/reduce_scatter | solution.py:82
  (130 shorter events, 82.4 us)
Async XLA Ops:
  7.2 120.0 %copy-start = (bf16[256,256]{1,0:T(8,128)(2,1)S(1)}, bf16[256,256]{1,0:T(8,128)(2,1)}, u32[]{:S(2)}) copy-start(bf16[256,256]{1,0:T(8,128)(2,1)} %param.15) | copy-start | bytes 393220
  7.2 45.8 %all-gather.2.cloned.1.call-start = ((), (), s32[]{:S(2)}) async-start(), calls=%async_computation.2 | async-start | bytes 1179648 | tf_op jit(solution)/shard_map/all_gather | solution.py:46
  7.9 119.2 %reduce-scatter.3.cloned.1.call-start = ((), (), s32[]{:S(2)}) async-start(), calls=%async_computation.3 | async-start | bytes 655360 | tf_op jit(solution)/shard_map/reduce_scatter | solution.py:58
  106.6 4.8 %copy-start.1 = (bf16[256,256]{1,0:T(8,128)(2,1)S(1)}, bf16[256,256]{1,0:T(8,128)(2,1)}, u32[]{:S(2)}) copy-start(bf16[256,256]{1,0:T(8,128)(2,1)} %param.13) | copy-start | bytes 393220
  106.6 4.8 %copy-start.2 = (bf16[256,256]{1,0:T(8,128)(2,1)S(1)}, bf16[256,256]{1,0:T(8,128)(2,1)}, u32[]{:S(2)}) copy-start(bf16[256,256]{1,0:T(8,128)(2,1)} %param.14) | copy-start | bytes 393220
  106.6 20.5 %copy-start.4 = (bf16[256,256]{1,0:T(8,128)(2,1)S(1)}, bf16[256,256]{1,0:T(8,128)(2,1)}, u32[]{:S(2)}) copy-start(bf16[256,256]{1,0:T(8,128)(2,1)} %param.17) | copy-start | bytes 393220
  106.6 20.5 %copy-start.5 = (f32[256]{0:T(256)S(1)}, f32[256]{0:T(256)}, u32[]{:S(2)}) copy-start(f32[256]{0:T(256)} %param.16) | copy-start | bytes 3076
  106.6 160.0 %all-reduce.3.cloned.1.call-start = ((), (), s32[]{:S(2)}) async-start(), calls=%async_computation.5 | async-start | bytes 1048576 | tf_op jit(solution)/shard_map/psum | solution.py:64
  127.1 9.9 %copy-start.3 = (bf16[256,256]{1,0:T(8,128)(2,1)S(1)}, bf16[256,256]{1,0:T(8,128)(2,1)}, u32[]{:S(2)}) copy-start(bf16[256,256]{1,0:T(8,128)(2,1)} %reduce-scatter.3.cloned.1.call-done) | copy-start | bytes 393220
  138.0 194.5 %reduce-scatter.5.cloned.1.call-start = ((), (), s32[]{:S(2)}) async-start(), calls=%async_computation.4 | async-start | bytes 1179648 | tf_op jit(solution)/shard_map/reduce_scatter | solution.py:82
Sparse Core Ops, SparseCore 0:
  10.1 42.8 all-gather.1
  106.7 20.3 reduce-scatter.2
  138.1 128.5 all-reduce.2
  269.9 62.4 reduce-scatter.4
where the time goes:
time: 345 us; the launch traced here: 342 us
  waiting for transfers between devices  147 us (43%)
  other arithmetic  76.1 us (22%)
  blocking collectives  46.6 us (14%)
  local copies, waits for them, and re-layouts  29.3 us (8%)
  matrix products  28.9 us (8%)
  between operations  13.9 us (4%)
    reduce_scatter x1, waiting for transfers between devices, local(): lax.psum_scatter(lax.fori_loop(0, nblocks, column_one_block, start_acc).r...  64 us
    all_gather x1, waiting for transfers between devices, local(): piece = lax.all_gather(features, 'blk', axis=0, tiled=True)  44.3 us
    psum x1, blocking collectives, local(): lax.psum((jnp.einsum('nf,ng->fg', features, grad_z, preferred_element_typ...  39.8 us
    scatter-add x8, other arithmetic, column_one_block(): return acc.at[j * per_dev + cols_here].add(term)  34.3 us
    psum x1, waiting for transfers between devices, local(): lax.psum((jnp.einsum('nf,ng->fg', features, grad_z, preferred_element_typ...  22.4 us
    reduce_scatter x1, waiting for transfers between devices, local(): lax.psum_scatter(partial_value.astype(jnp.bfloat16), 'rep', scatter_dimen...  15.5 us
    scatter-add x8, other arithmetic, add_one_block(): return acc.at[rows_here].add(prod)  14.7 us
    gather x8, local copies, waits for them, and re-layouts, add_one_block(): picked = jnp.take(tiles, j * per_dev + cols_here, axis=0)  14.6 us
  transfers between devices with their start and end apart: 4, of which 4 were waited for; matrix products, arithmetic and copies ran while one was open for 22% of the time, Pallas kernels for 0%

commit v1 on v0

v1 whole, which is shorter than its diff:
```python
import functools

import jax
import jax.numpy as jnp
from jax import lax
from jax.experimental import pallas as pl
from jax.experimental.pallas import tpu as pltpu
from jax.sharding import PartitionSpec as P

MESH = pl.DeviceIdType.MESH
F32 = jnp.float32
BF16 = jnp.bfloat16
PAD = 16


def dot_nn(a, b):
    return jnp.dot(a, b, preferred_element_type=F32)


def dot_nt(a, b):
    return lax.dot_general(a, b, (((1,), (1,)), ((), ())), preferred_element_type=F32)


def dot_tn(a, b):
    return lax.dot_general(a, b, (((0,), (0,)), ((), ())), preferred_element_type=F32)


def kernel(
    cfg,
    place_ref,
    x_ref,
    ws_ref,
    wn_ref,
    bias_ref,
    cot_ref,
    values_ref,
    out_ref,
    gradf_ref,
    gs_ref,
    gn_ref,
    gb_ref,
    vals,
    dense,
    xg,
    acc,
    zself,
    zsend,
    s1_recv,
    ysend,
    s2_recv,
    dg,
    yrecv,
    zrecv,
    gown,
    ga_send,
    ga_recv,
    gb_buf,
    gb_send,
    gc_buf,
    gc_send,
    gd_buf,
    ge_buf,
    vals_sem,
    x_rsem,
    x_ssem,
    s1_sems,
    s2_sems,
    dg_rsem,
    dg_ssem,
    y_sems,
    z_ssem,
    z_rsem,
    ga_sems,
    gb_sems,
    gc_sems,
    gd_sems,
    ge_sems,
    gf_sems,
):
    nblk, nrep, slots, tile, rows, width, scatter = cfg
    nz, chips = nblk // 2, nrep // 2
    per_dev = rows // tile
    rtiles = nrep * per_dev
    blk = lax.axis_index("blk")
    rep = lax.axis_index("rep")
    z, y = blk // 2, lax.rem(blk, 2)
    chip, core = rep // 2, lax.rem(rep, 2)
    oy, oc = 1 - y, 1 - core

    pending = []

    def send(src, dst, ssem, rsem, to_blk, to_rep, cond=None):
        copy = pltpu.make_async_remote_copy(
            src_ref=src,
            dst_ref=dst,
            send_sem=ssem,
            recv_sem=rsem,
            device_id=(to_blk, to_rep),
            device_id_type=MESH,
        )
        if cond is None:
            copy.start()
        else:
            pl.when(cond)(copy.start)
        pending.append((cond, copy))

    def arrived(dst, ssem, rsem):
        pltpu.make_async_remote_copy(
            src_ref=dst,
            dst_ref=dst,
            send_sem=ssem,
            recv_sem=rsem,
            device_id=(blk, rep),
            device_id_type=MESH,
        ).wait_recv()

    load = pltpu.make_async_copy(values_ref, vals.at[pl.ds(0, nblk * slots)], vals_sem)
    load.start()

    barrier = pltpu.get_barrier_semaphore()
    for i in range(1, nblk):
        pl.semaphore_signal(
            barrier, inc=1, device_id=(lax.rem(blk + i, nblk), rep), device_id_type=MESH
        )
    for i in range(1, nrep):
        pl.semaphore_signal(
            barrier, inc=1, device_id=(blk, lax.rem(rep + i, nrep)), device_id_type=MESH
        )
    pl.semaphore_wait(barrier, nblk + nrep - 2)

    def pass_on(src, origin, step, up, down):
        if up is not None:
            send(src, xg.at[origin], x_ssem.at[3 * step], x_rsem.at[origin], blk + 2, rep, up)
        if down is not None:
            send(src, xg.at[origin], x_ssem.at[3 * step + 1], x_rsem.at[origin], blk - 2, rep, down)

    def across(src, origin, sem_at, cond=None):
        send(src, xg.at[origin], x_ssem.at[sem_at], x_rsem.at[origin], z * 2 + oy, rep, cond)

    pass_on(x_ref, blk, 0, z < nz - 1, z > 0)
    across(x_ref, blk, 2)
    xg[blk] = x_ref[...]

    zself[...] = dot_nn(x_ref[...], ws_ref[...]) + bias_ref[...]
    vals[nblk * slots] = jnp.zeros((tile, tile), BF16)
    load.wait()

    def place_tiles(c, carry):
        def place_row(r):
            for t in range(per_dev):
                dense[c, pl.ds(r * tile, tile), t * tile : (t + 1) * tile] = vals[
                    place_ref[c, r * per_dev + t]
                ]

        if rtiles <= 8:
            for r in range(rtiles):
                place_row(r)
        else:
            pl.loop(0, rtiles)(place_row)
        return carry

    lax.fori_loop(0, nblk, place_tiles, 0)

    chunk = nrep * rows if nrep <= 4 else rows

    def add_block(c, first=False):
        def part(i):
            at = pl.ds(i * chunk, chunk)
            prod = dot_nn(dense[c, at, :], xg[c])
            if first:
                acc[at, :] = prod
            else:
                acc[at, :] += prod

        count = nrep * rows // chunk
        if count == 1:
            part(0)
        else:
            pl.loop(0, count)(part)

    add_block(blk, True)

    sem_base = 3 * nz
    for t in range(1, nz + 1):
        low, high = z - t, z + t
        if t < nz:
            olow, ohigh = low * 2 + y, high * 2 + y

            @pl.when(low >= 0)
            def _():
                arrived(xg.at[olow], x_ssem.at[0], x_rsem.at[olow])

            pass_on(xg.at[olow], olow, t, jnp.logical_and(low >= 0, z < nz - 1), None)
            across(xg.at[olow], olow, sem_base + 2 * t, low >= 0)

            @pl.when(high < nz)
            def _():
                arrived(xg.at[ohigh], x_ssem.at[0], x_rsem.at[ohigh])

            pass_on(xg.at[ohigh], ohigh, t, None, jnp.logical_and(high < nz, z > 0))
            across(xg.at[ohigh], ohigh, sem_base + 2 * t + 1, high < nz)

            @pl.when(low >= 0)
            def _():
                add_block(olow)

            @pl.when(high < nz)
            def _():
                add_block(ohigh)

        if t == 1:
            other = z * 2 + oy
            arrived(xg.at[other], x_ssem.at[0], x_rsem.at[other])
            add_block(other)
        else:
            plow, phigh = (z - (t - 1)) * 2 + oy, (z + (t - 1)) * 2 + oy

            @pl.when(z - (t - 1) >= 0)
            def _():
                arrived(xg.at[plow], x_ssem.at[0], x_rsem.at[plow])
                add_block(plow)

            @pl.when(z + (t - 1) < nz)
            def _():
                arrived(xg.at[phigh], x_ssem.at[0], x_rsem.at[phigh])
                add_block(phigh)

    mate = chip * 2 + oc
    before = len(pending)
    for i in range(chips):
        to = lax.rem(chip + 1 + i, chips)
        zsend[to] = acc[pl.ds((to * 2 + oc) * rows, rows), :].astype(BF16)
        send(zsend.at[to], s1_recv.at[to], s1_sems.at[0, to], s1_sems.at[1, to], blk, mate)
    total = None
    for i in range(chips):
        to = lax.rem(chip + 1 + i, chips)
        arrived(s1_recv.at[to], s1_sems.at[0, 0], s1_sems.at[1, to])
        part = acc[pl.ds((to * 2 + core) * rows, rows), :] + s1_recv[to].astype(F32)
        if i < chips - 1:
            ysend[to] = part.astype(BF16)
            send(
                ysend.at[to],
                s2_recv.at[chip],
                s2_sems.at[0, to],
                s2_sems.at[1, chip],
                blk,
                to * 2 + core,
            )
        else:
            total = part
    for i in range(chips - 1):
        frm = lax.rem(chip + 1 + i, chips)
        arrived(s2_recv.at[frm], s2_sems.at[0, 0], s2_sems.at[1, frm])
        total = total + s2_recv[frm].astype(F32)
    agg = total.astype(BF16)
    rep_sends = len(pending)

    zvals = zself[...] + dot_nn(agg, wn_ref[...])
    sig = jax.nn.sigmoid(zvals)
    out_ref[...] = (zvals * sig).astype(BF16)
    dz = (cot_ref[...].astype(F32) * sig * (1.0 + zvals * (1.0 - sig))).astype(BF16)
    dg[rep] = dot_nt(wn_ref[...], dz).astype(BF16)

    for i in range(chips - 1):
        to = lax.rem(chip + 1 + i, chips) * 2 + core
        send(dg.at[rep], dg.at[rep], dg_ssem.at[i], dg_rsem.at[rep], blk, to)
    send(dg.at[rep], dg.at[rep], dg_ssem.at[chips], dg_rsem.at[rep], blk, mate)

    gown[0] = dot_tn(x_ref[...], dz)
    gown[1] = dot_tn(agg, dz)
    gbias = jnp.broadcast_to(jnp.sum(dz.astype(F32), axis=0, keepdims=True), (PAD, width))
    ga_send[0:width, :] = gown[oc].astype(BF16)
    ga_send[width : width + PAD, :] = gbias.astype(BF16)
    send(ga_send, ga_recv, ga_sems.at[0], ga_sems.at[1], blk, mate)
    own = dot_nt(dz, ws_ref[...])

    for i in range(chips - 1):
        frm = lax.rem(chip + 1 + i, chips) * 2 + core
        arrived(dg.at[frm], dg_ssem.at[0], dg_rsem.at[frm])
        send(dg.at[frm], dg.at[frm], dg_ssem.at[chips + 1 + i], dg_rsem.at[frm], blk, mate)
    for i in range(chips):
        frm = lax.rem(chip + i, chips) * 2 + oc
        arrived(dg.at[frm], dg_ssem.at[0], dg_rsem.at[frm])

    for _, copy in pending[before:rep_sends]:
        copy.wait_send()
    del pending[before:rep_sends]

    def term(c):
        if nrep <= 4:
            out = dot_nn(dg[0], dense[c, 0:rows, :])
            for q in range(1, nrep):
                out = out + dot_nn(dg[q], dense[c, q * rows : (q + 1) * rows, :])
            return out

        def step(q, out):
            return out + dot_nn(dg[q], dense[c, pl.ds(q * rows, rows), :])

        return lax.fori_loop(0, nrep, step, jnp.zeros((width, rows), F32))

    def y_copy(dest):
        return pltpu.make_async_remote_copy(
            src_ref=ysend.at[dest],
            dst_ref=yrecv.at[dest],
            send_sem=y_sems.at[0, dest],
            recv_sem=y_sems.at[1, dest],
            device_id=(z * 2 + oy, rep),
            device_id_type=MESH,
        )

    turn = jnp.where(z < nz // 2, nz - 1, 1)

    def send_y(i, carry):
        dest = lax.rem(z + turn * (i + 1), nz)
        ysend[dest] = term(dest * 2 + oy).astype(BF16)
        y_copy(dest).start()
        return carry

    lax.fori_loop(0, nz, send_y, 0)

    def own_term(i, carry):
        acc[pl.ds(i * width, width), :] = term(i * 2 + y)
        return carry

    lax.fori_loop(0, nz, own_term, 0)

    arrived(ga_recv, ga_sems.at[0], ga_sems.at[1])
    share = width // scatter
    mine = gown[core] + ga_recv[0:width, :].astype(F32)
    gbias = gbias.astype(BF16).astype(F32) + ga_recv[width : width + PAD, :].astype(F32)
    gown[0] = mine
    if scatter == 1:
        gb_buf[chip, 0:share, :] = mine.astype(BF16)
    else:
        gb_buf[chip, 0:share, :] = gown[0, pl.ds(chip * share, share), :].astype(BF16)
    gb_buf[chip, share : share + PAD, :] = gbias.astype(BF16)
    for i in range(chips - 1):
        to = lax.rem(chip + 1 + i, chips)
        if scatter == 1:
            gb_send[i, 0:share, :] = mine.astype(BF16)
        else:
            gb_send[i, 0:share, :] = gown[0, pl.ds(to * share, share), :].astype(BF16)
        gb_send[i, share : share + PAD, :] = gbias.astype(BF16)
        send(
            gb_send.at[i],
            gb_buf.at[chip],
            gb_sems.at[0, i],
            gb_sems.at[1, chip],
            blk,
            to * 2 + core,
        )

    piece = share // nblk

    def grad_chips():
        for i in range(chips - 1):
            frm = lax.rem(chip + 1 + i, chips)
            arrived(gb_buf.at[frm], gb_sems.at[0, 0], gb_sems.at[1, frm])
        tot = gb_buf[0].astype(F32)
        for i in range(1, chips):
            tot = tot + gb_buf[i].astype(F32)
        for b in range(nblk):
            gc_send[b, 0:piece, :] = tot[b * piece : (b + 1) * piece].astype(BF16)
            gc_send[b, piece : piece + PAD, :] = tot[share : share + PAD].astype(BF16)
        gc_buf[blk] = gc_send[blk]
        for i in range(1, nblk):
            to = lax.rem(blk + i, nblk)
            send(gc_send.at[to], gc_buf.at[blk], gc_sems.at[0, to], gc_sems.at[1, blk], to, rep)

    def grad_blocks():
        for i in range(1, nblk):
            frm = lax.rem(blk + i, nblk)
            arrived(gc_buf.at[frm], gc_sems.at[0, 0], gc_sems.at[1, frm])
        tot = gc_buf[0].astype(F32)
        for b in range(1, nblk):
            tot = tot + gc_buf[b].astype(F32)
        gb_ref[...] = tot[piece : piece + 1]
        gd_buf[blk] = tot[0:piece].astype(BF16)
        for i in range(1, nblk):
            to = lax.rem(blk + i, nblk)
            send(gd_buf.at[blk], gd_buf.at[blk], gd_sems.at[0, to], gd_sems.at[1, blk], to, rep)

    def grad_back_blocks():
        for i in range(1, nblk):
            frm = lax.rem(blk + i, nblk)
            arrived(gd_buf.at[frm], gd_sems.at[0, 0], gd_sems.at[1, frm])
        for b in range(nblk):
            ge_buf[core, pl.ds(chip_at * share + b * piece, piece), :] = gd_buf[b]
        here = ge_buf.at[core, pl.ds(chip_at * share, share)]
        if scatter > 1:
            for i in range(chips - 1):
                to = lax.rem(chip + 1 + i, chips) * 2 + core
                send(here, here, ge_sems.at[0, i], ge_sems.at[1, chip], blk, to)

    def grad_back_chips():
        if scatter > 1:
            for i in range(chips - 1):
                frm = lax.rem(chip + 1 + i, chips)
                there = ge_buf.at[core, pl.ds(frm * share, share)]
                arrived(there, ge_sems.at[0, 0], ge_sems.at[1, frm])
        send(ge_buf.at[core], ge_buf.at[core], gf_sems.at[0], gf_sems.at[1], blk, mate)

    chip_at = chip if scatter > 1 else 0
    stages = [grad_chips, grad_blocks, grad_back_blocks, grad_back_chips]

    def gather_term(dest, src_dir, has_more):
        arrived(yrecv.at[dest], y_sems.at[0, 0], y_sems.at[1, dest])
        acc[pl.ds(dest * width, width), :] += yrecv[dest].astype(F32)

        @pl.when(has_more)
        def _():
            arrived(zrecv.at[src_dir, dest], z_ssem.at[0], z_rsem.at[src_dir, dest])
            acc[pl.ds(dest * width, width), :] += zrecv[src_dir, dest].astype(F32)

        zsend[dest] = acc[pl.ds(dest * width, width), :].astype(BF16)

    def chain_up(k, cond):
        dest = nz - 1 - k
        cond = jnp.logical_and(cond, z < dest)

        @pl.when(cond)
        def _():
            gather_term(dest, 0, z > 0)

        send(
            zsend.at[dest],
            zrecv.at[0, dest],
            z_ssem.at[dest],
            z_rsem.at[0, dest],
            blk + 2,
            rep,
            cond,
        )

    def chain_down(k):
        dest = k
        cond = z > dest

        @pl.when(cond)
        def _():
            gather_term(dest, 1, z < nz - 1)

        send(
            zsend.at[dest],
            zrecv.at[1, dest],
            z_ssem.at[dest],
            z_rsem.at[1, dest],
            blk - 2,
            rep,
            cond,
        )

    for k in range(nz - 1):
        chain_up(k, z < nz // 2)
        chain_down(k)
        chain_up(k, z >= nz // 2)
        if stages:
            stages.pop(0)()

    arrived(yrecv.at[z], y_sems.at[0, 0], y_sems.at[1, z])
    acc[pl.ds(z * width, width), :] += yrecv[z].astype(F32)

    @pl.when(z > 0)
    def _():
        arrived(zrecv.at[0, z], z_ssem.at[0], z_rsem.at[0, z])
        acc[pl.ds(z * width, width), :] += zrecv[0, z].astype(F32)

    @pl.when(z < nz - 1)
    def _():
        arrived(zrecv.at[1, z], z_ssem.at[0], z_rsem.at[1, z])
        acc[pl.ds(z * width, width), :] += zrecv[1, z].astype(F32)

    while stages:
        stages.pop(0)()

    gradf_ref[...] = (own + acc[pl.ds(z * width, width), :].T).astype(BF16)

    arrived(ge_buf.at[oc], gf_sems.at[0], gf_sems.at[1])
    gs_ref[...] = ge_buf[0].astype(F32)
    gn_ref[...] = ge_buf[1].astype(F32)

    for cond, copy in pending:
        if cond is None:
            copy.wait_send()
        else:
            pl.when(cond)(copy.wait_send)

    def drain_y(i, carry):
        y_copy(i).wait_send()
        return carry

    lax.fori_loop(0, nz, drain_y, 0)


def local(
    features, w_self, w_neigh, bias, cotangent, tile_values, tile_rows, tile_cols, tile_counts
):
    rows, width = features.shape
    nblk, nrep = lax.axis_size("blk"), lax.axis_size("rep")
    slots, tile = tile_values.shape[3], tile_values.shape[4]
    per_dev = rows // tile
    places = nrep * per_dev * per_dev
    nz, chips = nblk // 2, nrep // 2
    scatter = chips if width % (chips * nblk * 16) == 0 else 1
    share = width // scatter
    piece = share // nblk

    slot_place = tile_rows[0, 0] * per_dev + tile_cols[0, 0]
    slot_ids = lax.broadcasted_iota(jnp.int32, (nblk, slots), 1)
    slot_place = jnp.where(slot_ids < tile_counts[0, 0][:, None], slot_place, -1)
    flat = lax.broadcasted_iota(jnp.int32, (nblk, slots), 0) * slots + slot_ids
    empty = nblk * slots
    hit = slot_place[:, :, None] == lax.broadcasted_iota(jnp.int32, (1, 1, places), 2)
    place = empty + jnp.sum(jnp.where(hit, flat[:, :, None] - empty, 0), axis=1)

    cfg = (nblk, nrep, slots, tile, rows, width, scatter)
    vmem = pl.BlockSpec(memory_space=pltpu.VMEM)
    sems = pltpu.SemaphoreType.DMA
    outs = pl.pallas_call(
        functools.partial(kernel, cfg),
        out_shape=(
            jax.ShapeDtypeStruct((rows, width), BF16),
            jax.ShapeDtypeStruct((rows, width), BF16),
            jax.ShapeDtypeStruct((width, width), F32),
            jax.ShapeDtypeStruct((width, width), F32),
            jax.ShapeDtypeStruct((1, width), F32),
        ),
        in_specs=[
            pl.BlockSpec(memory_space=pltpu.SMEM),
            vmem,
            vmem,
            vmem,
            vmem,
            vmem,
            pl.BlockSpec(memory_space=pl.ANY),
        ],
        out_specs=(vmem,) * 5,
        scratch_shapes=[
            pltpu.VMEM((nblk * slots + 1, tile, tile), BF16),
            pltpu.VMEM((nblk, nrep * rows, rows), BF16),
            pltpu.VMEM((nblk, rows, width), BF16),
            pltpu.VMEM((max(nrep * rows, nz * width), width), F32),
            pltpu.VMEM((rows, width), F32),
            pltpu.VMEM((max(chips, nz), rows, width), BF16),
            pltpu.VMEM((chips, rows, width), BF16),
            pltpu.VMEM((max(chips, nz), rows, width), BF16),
            pltpu.VMEM((chips, rows, width), BF16),
            pltpu.VMEM((nrep, width, rows), BF16),
                pltpu.VMEM((nz, width, rows), BF16),
            pltpu.VMEM((2, nz, width, rows), BF16),
            pltpu.VMEM((2, width, width), F32),
            pltpu.VMEM((width + PAD, width), BF16),
            pltpu.VMEM((width + PAD, width), BF16),
            pltpu.VMEM((chips, share + PAD, width), BF16),
            pltpu.VMEM((chips, share + PAD, width), BF16),
            pltpu.VMEM((nblk, piece + PAD, width), BF16),
            pltpu.VMEM((nblk, piece + PAD, width), BF16),
            pltpu.VMEM((nblk, piece, width), BF16),
            pltpu.VMEM((2, width, width), BF16),
            sems,
            sems((nblk,)),
            sems((5 * nz,)),
            sems((2, chips)),
            sems((2, chips)),
            sems((nrep,)),
            sems((2 * chips + 1,)),
            sems((2, nz)),
            sems((nz,)),
            sems((2, nz)),
            sems((2,)),
            sems((2, chips)),
            sems((2, nblk)),
            sems((2, nblk)),
            sems((2, chips)),
            sems((2,)),
        ],
        compiler_params=pltpu.CompilerParams(
            collective_id=0, has_side_effects=True, vmem_limit_bytes=60 * 1024 * 1024
        ),
        cost_estimate=pl.CostEstimate(
            flops=4 * nblk * nrep * rows * rows * width,
            bytes_accessed=nblk * slots * tile * tile * 2,
            transcendentals=rows * width,
        ),
    )(
        place,
        features,
        w_self,
        w_neigh,
        bias.reshape(1, width),
        cotangent,
        tile_values.reshape(nblk * slots, tile, tile),
    )
    output, grad_features, grad_self, grad_neigh, grad_bias = outs
    return output, grad_features, grad_self, grad_neigh, grad_bias.reshape(width)


def solution(mesh):
    in_specs = (
        P(("blk", "rep"), None),
        P(),
        P(),
        P(),
        P(("blk", "rep"), None),
        P("blk", "rep", None, None, None, None),
        P("blk", "rep", None, None),
        P("blk", "rep", None, None),
        P("blk", "rep", None),
    )
    out_specs = (P(("blk", "rep"), None), P(("blk", "rep"), None), P(), P(), P())
    return jax.shard_map(local, mesh=mesh, in_specs=in_specs, out_specs=out_specs, check_vma=False)
```

time: 345 us -> 77 us (0.22)
  waiting for transfers between devices: 147 us -> 0 us
  other arithmetic: 76.1 us -> 1.47 us
  Pallas kernels: 0 us -> 66.8 us
  blocking collectives: 46.6 us -> 0 us
  matrix products: 28.9 us -> 0 us
  local copies, waits for them, and re-layouts: 29.3 us -> 7.78 us
  between operations: 13.9 us -> 0.66 us
    reduce_scatter x2 -> x0, waiting for transfers between devices: 79.5 us -> none  [the longest x1 64 us: local(): lax.psum_scatter(lax.fori_loop(0, nblocks, column_one_block, start_acc).r...]
    pallas_call x0 -> x1, Pallas kernels: none -> 66.8 us  [local(): pl.pallas_call(functools.partial(kernel, cfg), out_shape=(jax.ShapeDtypeS...]
    scatter-add x16 -> x0, other arithmetic: 49 us -> none  [the longest x8 34.3 us: column_one_block(): return acc.at[j * per_dev + cols_here].add(term)]
    all_gather x1 -> x0, waiting for transfers between devices: 44.3 us -> none  [local(): piece = lax.all_gather(features, 'blk', axis=0, tiled=True)]
    psum x1 -> x0, blocking collectives: 39.8 us -> none  [local(): lax.psum((jnp.einsum('nf,ng->fg', features, grad_z, preferred_element_typ...]
    dot_general x22 -> x0, matrix products: 28.9 us -> none  [the longest x8 11.5 us: column_one_block(): jnp.einsum('sji,sjf->sif', vals, picked, preferred_element_type=jnp.float32)]
    psum x1 -> x0, waiting for transfers between devices: 22.4 us -> none  [local(): lax.psum((jnp.einsum('nf,ng->fg', features, grad_z, preferred_element_typ...]
    gather x16 -> x0, local copies, waits for them, and re-layouts: 19.3 us -> none  [the longest x8 14.6 us: add_one_block(): picked = jnp.take(tiles, j * per_dev + cols_here, axis=0)]
  transfers between devices with their start and end apart: 4 -> 0, of which waited for: 4 -> 0; matrix products, arithmetic and copies ran while one was open for 22% -> 0% of each run, Pallas kernels for 0% -> 0%
where the time goes in v1:
time: 77 us; the launch traced here: 76.7 us
  Pallas kernels  66.8 us (87%)
  local copies, waits for them, and re-layouts  7.78 us (10%)
  other arithmetic  1.47 us (2%)
    pallas_call x1, Pallas kernels, local(): pl.pallas_call(functools.partial(kernel, cfg), out_shape=(jax.ShapeDtypeS...  66.8 us
    unnamed x5, local copies, waits for them, and re-layouts  7.7 us

profile of v1, /device:TPU:0, one launch (start us, length us, event | category | flops | bytes accessed | tf_op | source)
XLA Modules:
  0.0 76.7 jit_solution(4437600271429189665)
XLA Ops:
  0.6 0.8 %bitcast_select_fusion = s32[8,12]{1,0:T(8,128)S(1)} fusion(s32[1,1,8,12]{3,2,1,0:T(8,128)} %param.16, s32[1,1,8,12]{3,2,1,0:T(8,128)} %param.15, s32[8]{0:T(128)} %bitcast.7), kind=kLoop, calls=%fused_computation.3 | loop fusion | flops 384 | bytes 1184 | tf_op jit(solution)/shard_map/jit(_where)/select_n | solution.py:510
  1.4 0.1 copy.14
  1.5 0.1 select_reduce_fusion
  1.6 0.6 broadcast_add_fusion.place_ref
  2.2 66.8 %shard_map.128 = (bf16[256,256]{1,0:T(8,128)(2,1)}, bf16[256,256]{1,0:T(8,128)(2,1)}, f32[256,256]{1,0:T(8,128)}, f32[256,256]{1,0:T(8,128)}, f32[1,256]{1,0:T(1,128)}) custom-call(s32[8,16]{1,0:T(8,128)} %broadcast_add_fusion.place_ref, bf16[256,256]{1,0:T(8,128)(2,1)} %x_ref.1, bf16[256,256]{1,0:T(8,128)(2,1)} %ws_ref.1, bf16[256,256]{1,0:T(8,128)(2,1)} %wn_ref.1, ...), custom_call_target="tpu_custom_call" | custom-call | flops 2147483648 | bytes 3145728 | tf_op jit(solution)/shard_map/pallas_call | solution.py:519
  69.0 1.6 %copy.20 = bf16[256,256]{1,0:T(8,128)(2,1)} copy(bf16[256,256]{1,0:T(8,128)(2,1)} %get-tuple-element.20) | data formatting | bytes 262144
  70.6 1.6 %copy.21 = bf16[256,256]{1,0:T(8,128)(2,1)} copy(bf16[256,256]{1,0:T(8,128)(2,1)} %get-tuple-element.21) | data formatting | bytes 262144
  72.1 1.7 %copy.22 = f32[256,256]{1,0:T(8,128)} copy(f32[256,256]{1,0:T(8,128)} %get-tuple-element.22) | data formatting | bytes 524288
  73.8 1.7 %copy.23 = f32[256,256]{1,0:T(8,128)} copy(f32[256,256]{1,0:T(8,128)} %get-tuple-element.23) | data formatting | bytes 524288
  75.5 1.2 %copy.24 = f32[256]{0:T(256)} copy(f32[256]{0:T(256)} %bitcast.6) | data formatting | bytes 2048
  (2 shorter events, 0.0 us)

commit v2 on v1

v2 whole, which is shorter than its diff:
```python
import functools

import jax
import jax.numpy as jnp
from jax import lax
from jax.experimental import pallas as pl
from jax.experimental.pallas import tpu as pltpu
from jax.sharding import PartitionSpec as P

MESH = pl.DeviceIdType.MESH
F32 = jnp.float32
BF16 = jnp.bfloat16
PAD = 16


def dot_nn(a, b):
    return jnp.dot(a, b, preferred_element_type=F32)


def dot_nt(a, b):
    return lax.dot_general(a, b, (((1,), (1,)), ((), ())), preferred_element_type=F32)


def dot_tn(a, b):
    return lax.dot_general(a, b, (((0,), (0,)), ((), ())), preferred_element_type=F32)


def kernel(
    cfg,
    place_ref,
    x_ref,
    ws_ref,
    wn_ref,
    bias_ref,
    cot_ref,
    values_ref,
    out_ref,
    gradf_ref,
    ge_ref,
    gb_ref,
    vals,
    dense,
    xg,
    acc,
    zself,
    zsend,
    s1_recv,
    ysend,
    s2_recv,
    dg,
    yrecv,
    zrecv,
    gown,
    ga_send,
    ga_recv,
    gb_buf,
    gc_buf,
    gc_send,
    ge_buf,
    vals_sem,
    x_rsem,
    x_ssem,
    s1_sems,
    s2_sems,
    dg_rsem,
    dg_ssem,
    y_sems,
    z_ssem,
    z_rsem,
    ga_sems,
    gb_sems,
    gc_sems,
    gd_sems,
    gf_sems,
):
    nblk, nrep, slots, tile, rows, width = cfg
    nz, chips = nblk // 2, nrep // 2
    per_dev = rows // tile
    rtiles = nrep * per_dev
    blk = lax.axis_index("blk")
    rep = lax.axis_index("rep")
    z, y = blk // 2, lax.rem(blk, 2)
    chip, core = rep // 2, lax.rem(rep, 2)
    oy, oc = 1 - y, 1 - core

    pending = []

    def send(src, dst, ssem, rsem, to_blk, to_rep, cond=None):
        copy = pltpu.make_async_remote_copy(
            src_ref=src,
            dst_ref=dst,
            send_sem=ssem,
            recv_sem=rsem,
            device_id=(to_blk, to_rep),
            device_id_type=MESH,
        )
        if cond is None:
            copy.start()
        else:
            pl.when(cond)(copy.start)
        pending.append((cond, copy))

    def arrived(dst, ssem, rsem):
        pltpu.make_async_remote_copy(
            src_ref=dst,
            dst_ref=dst,
            send_sem=ssem,
            recv_sem=rsem,
            device_id=(blk, rep),
            device_id_type=MESH,
        ).wait_recv()

    load = pltpu.make_async_copy(values_ref, vals.at[pl.ds(0, nblk * slots)], vals_sem)
    load.start()

    barrier = pltpu.get_barrier_semaphore()
    for i in range(1, nblk):
        pl.semaphore_signal(
            barrier, inc=1, device_id=(lax.rem(blk + i, nblk), rep), device_id_type=MESH
        )
    for i in range(1, nrep):
        pl.semaphore_signal(
            barrier, inc=1, device_id=(blk, lax.rem(rep + i, nrep)), device_id_type=MESH
        )
    pl.semaphore_wait(barrier, nblk + nrep - 2)

    half = rows // 2

    def pass_on(src, origin, step, h, kind, to_blk, cond):
        send(
            src.at[pl.ds(h * half, half)],
            xg.at[origin, pl.ds(h * half, half)],
            x_ssem.at[step, h, kind],
            x_rsem.at[origin, h],
            to_blk,
            rep,
            cond,
        )

    def half_arrived(origin, h):
        arrived(xg.at[origin, pl.ds(h * half, half)], x_ssem.at[0, 0, 0], x_rsem.at[origin, h])

    for h in range(2):
        pass_on(x_ref, blk, 0, h, 0, blk + 2, z < nz - 1)
        pass_on(x_ref, blk, 0, h, 1, blk - 2, z > 0)
        pass_on(x_ref, blk, 0, h, 2, z * 2 + oy, None)
    xg[blk] = x_ref[...]

    zself[...] = dot_nn(x_ref[...], ws_ref[...]) + bias_ref[...]
    vals[nblk * slots] = jnp.zeros((tile, tile), BF16)
    load.wait()

    def place_tiles(c, carry):
        def place_row(r):
            for t in range(per_dev):
                dense[c, pl.ds(r * tile, tile), t * tile : (t + 1) * tile] = vals[
                    place_ref[c, r * per_dev + t]
                ]

        if rtiles <= 8:
            for r in range(rtiles):
                place_row(r)
        else:
            pl.loop(0, rtiles)(place_row)
        return carry

    lax.fori_loop(0, nblk, place_tiles, 0)

    chunk = nrep * rows if nrep <= 4 else rows

    def add_block(c, first=False):
        def part(i):
            at = pl.ds(i * chunk, chunk)
            prod = dot_nn(dense[c, at, :], xg[c])
            if first:
                acc[at, :] = prod
            else:
                acc[at, :] += prod

        count = nrep * rows // chunk
        if count == 1:
            part(0)
        else:
            pl.loop(0, count)(part)

    add_block(blk, True)

    def add_pair(step, side, wait):
        for at in (z - step, z + step):
            origin = at * 2 + side

            @pl.when(jnp.logical_and(at >= 0, at < nz))
            def _():
                if wait:
                    half_arrived(origin, 0)
                    half_arrived(origin, 1)
                add_block(origin)

    for t in range(1, nz):
        for h in range(2):
            for at, kind, inner in ((z - t, 0, z < nz - 1), (z + t, 1, z > 0)):
                origin = at * 2 + y
                there = at >= 0 if kind == 0 else at < nz
                on = blk + 2 if kind == 0 else blk - 2

                @pl.when(there)
                def _():
                    half_arrived(origin, h)

                held = xg.at[origin]
                pass_on(held, origin, t, h, kind, on, jnp.logical_and(there, inner))
                pass_on(held, origin, t, h, kind + 2, z * 2 + oy, there)
        add_pair(t, y, False)
        if t == 1:
            half_arrived(z * 2 + oy, 0)
            half_arrived(z * 2 + oy, 1)
            add_block(z * 2 + oy)
        else:
            add_pair(t - 1, oy, True)
    add_pair(nz - 1, oy, True)

    mate = chip * 2 + oc
    before = len(pending)
    for i in range(chips):
        to = lax.rem(chip + 1 + i, chips)
        zsend[to] = acc[pl.ds((to * 2 + oc) * rows, rows), :].astype(BF16)
        send(zsend.at[to], s1_recv.at[to], s1_sems.at[0, to], s1_sems.at[1, to], blk, mate)
    total = None
    for i in range(chips):
        to = lax.rem(chip + 1 + i, chips)
        arrived(s1_recv.at[to], s1_sems.at[0, 0], s1_sems.at[1, to])
        part = acc[pl.ds((to * 2 + core) * rows, rows), :] + s1_recv[to].astype(F32)
        if i < chips - 1:
            ysend[to] = part.astype(BF16)
            send(
                ysend.at[to],
                s2_recv.at[chip],
                s2_sems.at[0, to],
                s2_sems.at[1, chip],
                blk,
                to * 2 + core,
            )
        else:
            total = part
    for i in range(chips - 1):
        frm = lax.rem(chip + 1 + i, chips)
        arrived(s2_recv.at[frm], s2_sems.at[0, 0], s2_sems.at[1, frm])
        total = total + s2_recv[frm].astype(F32)
    agg = total.astype(BF16)
    rep_sends = len(pending)

    zvals = zself[...] + dot_nn(agg, wn_ref[...])
    sig = jax.nn.sigmoid(zvals)
    out_ref[...] = (zvals * sig).astype(BF16)
    dz = (cot_ref[...].astype(F32) * sig * (1.0 + zvals * (1.0 - sig))).astype(BF16)
    dg[rep] = dot_nt(wn_ref[...], dz).astype(BF16)

    for i in range(chips - 1):
        to = lax.rem(chip + 1 + i, chips) * 2 + core
        send(dg.at[rep], dg.at[rep], dg_ssem.at[i], dg_rsem.at[rep], blk, to)
    send(dg.at[rep], dg.at[rep], dg_ssem.at[chips], dg_rsem.at[rep], blk, mate)

    gown[0] = dot_tn(x_ref[...], dz)
    gown[1] = dot_tn(agg, dz)
    gbias = jnp.broadcast_to(jnp.sum(dz.astype(F32), axis=0, keepdims=True), (PAD, width))
    ga_send[0:width, :] = gown[oc].astype(BF16)
    ga_send[width : width + PAD, :] = gbias.astype(BF16)
    send(ga_send, ga_recv, ga_sems.at[0], ga_sems.at[1], blk, mate)
    own = dot_nt(dz, ws_ref[...])
    piece = width // nblk

    arrived(ga_recv, ga_sems.at[0], ga_sems.at[1])
    gbias = gbias.astype(BF16).astype(F32) + ga_recv[width : width + PAD, :].astype(F32)
    gown[0] = gown[core] + ga_recv[0:width, :].astype(F32)
    for b in range(nblk):
        gc_send[b, 0:piece, :] = gown[0, b * piece : (b + 1) * piece].astype(BF16)
        gc_send[b, piece : piece + PAD, :] = gbias.astype(BF16)
    gc_buf[blk] = gc_send[blk]
    for i in range(1, nblk):
        to = lax.rem(blk + i, nblk)
        send(gc_send.at[to], gc_buf.at[blk], gc_sems.at[0, to], gc_sems.at[1, blk], to, rep)

    for i in range(chips - 1):
        frm = lax.rem(chip + 1 + i, chips) * 2 + core
        arrived(dg.at[frm], dg_ssem.at[0], dg_rsem.at[frm])
        send(dg.at[frm], dg.at[frm], dg_ssem.at[chips + 1 + i], dg_rsem.at[frm], blk, mate)
    for i in range(chips):
        frm = lax.rem(chip + i, chips) * 2 + oc
        arrived(dg.at[frm], dg_ssem.at[0], dg_rsem.at[frm])

    for _, copy in pending[before:rep_sends]:
        copy.wait_send()
    del pending[before:rep_sends]

    def term(c):
        if nrep <= 4:
            out = dot_nn(dg[0], dense[c, 0:rows, :])
            for q in range(1, nrep):
                out = out + dot_nn(dg[q], dense[c, q * rows : (q + 1) * rows, :])
            return out

        def step(q, out):
            return out + dot_nn(dg[q], dense[c, pl.ds(q * rows, rows), :])

        return lax.fori_loop(0, nrep, step, jnp.zeros((width, rows), F32))

    fhalf = width // 2

    def y_copy(dest, h):
        at = pl.ds(h * fhalf, fhalf)
        return pltpu.make_async_remote_copy(
            src_ref=ysend.at[dest, at],
            dst_ref=yrecv.at[dest, at],
            send_sem=y_sems.at[0, dest, h],
            recv_sem=y_sems.at[1, dest, h],
            device_id=(z * 2 + oy, rep),
            device_id_type=MESH,
        )

    near = jnp.minimum(z, nz - 1 - z)

    def send_y(i, carry):
        dest = jnp.where(
            i < 2 * near,
            jnp.where(lax.rem(i, 2) == 0, nz - 1 - i // 2, i // 2),
            nz - 1 - (i - near),
        )
        dest = jnp.where(z < nz // 2, dest, nz - 1 - dest)
        ysend[dest] = term(dest * 2 + oy).astype(BF16)
        y_copy(dest, 0).start()
        y_copy(dest, 1).start()
        return carry

    lax.fori_loop(0, nz, send_y, 0)

    def own_term(i, carry):
        acc[pl.ds(i * width, width), :] = term(i * 2 + y)
        return carry

    lax.fori_loop(0, nz, own_term, 0)

    def grad_sums():
        for i in range(1, nblk):
            frm = lax.rem(blk + i, nblk)
            arrived(gc_buf.at[frm], gc_sems.at[0, 0], gc_sems.at[1, frm])
        tot = gc_buf[0].astype(F32)
        for b in range(1, nblk):
            tot = tot + gc_buf[b].astype(F32)
        gb_buf[chip] = tot.astype(BF16)
        for i in range(chips - 1):
            to = lax.rem(chip + 1 + i, chips)
            send(
                gb_buf.at[chip],
                gb_buf.at[chip],
                gb_sems.at[0, i],
                gb_sems.at[1, chip],
                blk,
                to * 2 + core,
            )
        for i in range(chips - 1):
            frm = lax.rem(chip + 1 + i, chips)
            arrived(gb_buf.at[frm], gb_sems.at[0, 0], gb_sems.at[1, frm])
        tot = gb_buf[0].astype(F32)
        for i in range(1, chips):
            tot = tot + gb_buf[i].astype(F32)
        gb_ref[...] = tot[piece : piece + 1]
        here = ge_buf.at[core, pl.ds(blk * piece, piece)]
        ge_buf[core, pl.ds(blk * piece, piece), :] = tot[0:piece].astype(BF16)
        for i in range(1, nblk):
            to = lax.rem(blk + i, nblk)
            send(here, here, gd_sems.at[0, to], gd_sems.at[1, blk], to, rep)

    def grad_back():
        for i in range(1, nblk):
            frm = lax.rem(blk + i, nblk)
            arrived(
                ge_buf.at[core, pl.ds(frm * piece, piece)], gd_sems.at[0, 0], gd_sems.at[1, frm]
            )
        send(ge_buf.at[core], ge_buf.at[core], gf_sems.at[0], gf_sems.at[1], blk, mate)

    def add_from(buf, dest, h, sem):
        at = pl.ds(dest * width + h * fhalf, fhalf)
        arrived(buf.at[pl.ds(h * fhalf, fhalf)], z_ssem.at[0, 0], sem)
        acc[at, :] += buf[h * fhalf : (h + 1) * fhalf, :].astype(F32)

    def chain(k, way, cond):
        dest = nz - 1 - k if way == 0 else k
        on = blk + 2 if way == 0 else blk - 2
        more = z > 0 if way == 0 else z < nz - 1
        cond = jnp.logical_and(cond, z < dest if way == 0 else z > dest)
        for h in range(2):

            @pl.when(cond)
            def _():
                add_from(yrecv.at[dest], dest, h, y_sems.at[1, dest, h])

                @pl.when(more)
                def _():
                    add_from(zrecv.at[way, dest], dest, h, z_rsem.at[way, dest, h])

                rows_at = pl.ds(dest * width + h * fhalf, fhalf)
                zsend[dest, h * fhalf : (h + 1) * fhalf, :] = acc[rows_at, :].astype(BF16)

            at = pl.ds(h * fhalf, fhalf)
            send(
                zsend.at[dest, at],
                zrecv.at[way, dest, at],
                z_ssem.at[dest, h],
                z_rsem.at[way, dest, h],
                on,
                rep,
                cond,
            )

    at_end = near == 0
    chain(0, 0, z == 0)
    chain(0, 1, z == nz - 1)
    grad_sums()
    for k in range(nz - 1):
        inside = z >= 0 if k else jnp.logical_not(at_end)
        chain(k, 0, jnp.logical_and(inside, z < nz // 2))
        chain(k, 1, inside)
        chain(k, 0, jnp.logical_and(inside, z >= nz // 2))

    grad_back()
    for h in range(2):
        add_from(yrecv.at[z], z, h, y_sems.at[1, z, h])

        @pl.when(z > 0)
        def _():
            add_from(zrecv.at[0, z], z, h, z_rsem.at[0, z, h])

        @pl.when(z < nz - 1)
        def _():
            add_from(zrecv.at[1, z], z, h, z_rsem.at[1, z, h])

    gradf_ref[...] = (own + acc[pl.ds(z * width, width), :].T).astype(BF16)

    arrived(ge_buf.at[oc], gf_sems.at[0], gf_sems.at[1])
    ge_ref[...] = ge_buf[...]

    for cond, copy in pending:
        if cond is None:
            copy.wait_send()
        else:
            pl.when(cond)(copy.wait_send)

    def drain_y(i, carry):
        y_copy(i, 0).wait_send()
        y_copy(i, 1).wait_send()
        return carry

    lax.fori_loop(0, nz, drain_y, 0)


def hand_out(a_ref, b_ref, c_ref, d_ref, out_ref, gradf_ref, gs_ref, gn_ref, gb_ref):
    out_ref[...] = a_ref[...]
    gradf_ref[...] = b_ref[...]
    gs_ref[...] = c_ref[0].astype(F32)
    gn_ref[...] = c_ref[1].astype(F32)
    gb_ref[...] = d_ref[...]


def local(
    features, w_self, w_neigh, bias, cotangent, tile_values, tile_rows, tile_cols, tile_counts
):
    rows, width = features.shape
    nblk, nrep = lax.axis_size("blk"), lax.axis_size("rep")
    slots, tile = tile_values.shape[3], tile_values.shape[4]
    per_dev = rows // tile
    places = nrep * per_dev * per_dev
    nz, chips = nblk // 2, nrep // 2
    piece = width // nblk

    slot_place = tile_rows[0, 0] * per_dev + tile_cols[0, 0]
    slot_ids = lax.broadcasted_iota(jnp.int32, (nblk, slots), 1)
    slot_place = jnp.where(slot_ids < tile_counts[0, 0][:, None], slot_place, -1)
    flat = lax.broadcasted_iota(jnp.int32, (nblk, slots), 0) * slots + slot_ids
    empty = nblk * slots
    hit = slot_place[:, :, None] == lax.broadcasted_iota(jnp.int32, (1, 1, places), 2)
    place = empty + jnp.sum(jnp.where(hit, flat[:, :, None] - empty, 0), axis=1)

    cfg = (nblk, nrep, slots, tile, rows, width)
    vmem = pl.BlockSpec(memory_space=pltpu.VMEM)
    sems = pltpu.SemaphoreType.DMA
    outs = pl.pallas_call(
        functools.partial(kernel, cfg),
        out_shape=(
            jax.ShapeDtypeStruct((rows, width), BF16),
            jax.ShapeDtypeStruct((rows, width), BF16),
            jax.ShapeDtypeStruct((2, width, width), BF16),
            jax.ShapeDtypeStruct((1, width), F32),
        ),
        in_specs=[
            pl.BlockSpec(memory_space=pltpu.SMEM),
            vmem,
            vmem,
            vmem,
            vmem,
            vmem,
            pl.BlockSpec(memory_space=pl.ANY),
        ],
        out_specs=(vmem,) * 4,
        scratch_shapes=[
            pltpu.VMEM((nblk * slots + 1, tile, tile), BF16),
            pltpu.VMEM((nblk, nrep * rows, rows), BF16),
            pltpu.VMEM((nblk, rows, width), BF16),
            pltpu.VMEM((max(nrep * rows, nz * width), width), F32),
            pltpu.VMEM((rows, width), F32),
            pltpu.VMEM((max(chips, nz), rows, width), BF16),
            pltpu.VMEM((chips, rows, width), BF16),
            pltpu.VMEM((max(chips, nz), rows, width), BF16),
            pltpu.VMEM((chips, rows, width), BF16),
            pltpu.VMEM((nrep, width, rows), BF16),
                pltpu.VMEM((nz, width, rows), BF16),
            pltpu.VMEM((2, nz, width, rows), BF16),
            pltpu.VMEM((2, width, width), F32),
            pltpu.VMEM((width + PAD, width), BF16),
            pltpu.VMEM((width + PAD, width), BF16),
            pltpu.VMEM((chips, piece + PAD, width), BF16),
            pltpu.VMEM((nblk, piece + PAD, width), BF16),
            pltpu.VMEM((nblk, piece + PAD, width), BF16),
            pltpu.VMEM((2, width, width), BF16),
            sems,
            sems((nblk, 2)),
            sems((nz, 2, 4)),
            sems((2, chips)),
            sems((2, chips)),
            sems((nrep,)),
            sems((2 * chips + 1,)),
            sems((2, nz, 2)),
            sems((nz, 2)),
            sems((2, nz, 2)),
            sems((2,)),
            sems((2, chips)),
            sems((2, nblk)),
            sems((2, nblk)),
            sems((2,)),
        ],
        compiler_params=pltpu.CompilerParams(
            collective_id=0, has_side_effects=True, vmem_limit_bytes=60 * 1024 * 1024
        ),
        cost_estimate=pl.CostEstimate(
            flops=4 * nblk * nrep * rows * rows * width,
            bytes_accessed=nblk * slots * tile * tile * 2,
            transcendentals=rows * width,
        ),
    )(
        place,
        features,
        w_self,
        w_neigh,
        bias.reshape(1, width),
        cotangent,
        tile_values.reshape(nblk * slots, tile, tile),
    )
    output, grad_features, grad_self, grad_neigh, grad_bias = pl.pallas_call(
        hand_out,
        out_shape=(
            jax.ShapeDtypeStruct((rows, width), BF16),
            jax.ShapeDtypeStruct((rows, width), BF16),
            jax.ShapeDtypeStruct((width, width), F32),
            jax.ShapeDtypeStruct((width, width), F32),
            jax.ShapeDtypeStruct((1, width), F32),
        ),
        in_specs=[vmem] * 4,
        out_specs=(vmem,) * 5,
    )(*outs)
    return output, grad_features, grad_self, grad_neigh, grad_bias.reshape(width)


def solution(mesh):
    in_specs = (
        P(("blk", "rep"), None),
        P(),
        P(),
        P(),
        P(("blk", "rep"), None),
        P("blk", "rep", None, None, None, None),
        P("blk", "rep", None, None),
        P("blk", "rep", None, None),
        P("blk", "rep", None),
    )
    out_specs = (P(("blk", "rep"), None), P(("blk", "rep"), None), P(), P(), P())
    return jax.shard_map(local, mesh=mesh, in_specs=in_specs, out_specs=out_specs, check_vma=False)
```

time: 77 us -> 57.3 us (0.74); the launches traced: 76.7 us -> 56.1 us
  Pallas kernels: 66.8 us -> 53.9 us
  local copies, waits for them, and re-layouts: 7.78 us -> 0.09 us
    pallas_call x1, Pallas kernels: 66.8 us -> 51.9 us  [local(): pl.pallas_call(functools.partial(kernel, cfg), out_shape=(jax.ShapeDtypeS...]
    unnamed x5 -> x0, local copies, waits for them, and re-layouts: 7.7 us -> none
    pallas_call x0 -> x1, Pallas kernels: none -> 1.98 us  [local(): pl.pallas_call(hand_out, out_shape=(jax.ShapeDtypeStruct((rows, width), B...]
where the time goes in v2:
time: 57.3 us; the launch traced here: 56.1 us
  Pallas kernels  53.9 us (94%)
  other arithmetic  1.47 us (3%)
  between operations  0.65 us (1%)
    pallas_call x1, Pallas kernels, local(): pl.pallas_call(functools.partial(kernel, cfg), out_shape=(jax.ShapeDtypeS...  51.9 us
    pallas_call x1, Pallas kernels, local(): pl.pallas_call(hand_out, out_shape=(jax.ShapeDtypeStruct((rows, width), B...  1.98 us

profile of v2, /device:TPU:0, one launch (start us, length us, event | category | flops | bytes accessed | tf_op | source)
XLA Modules:
  0.0 56.1 jit_solution(12504879572393476751)
XLA Ops:
  0.6 0.8 %bitcast_select_fusion = s32[8,12]{1,0:T(8,128)S(1)} fusion(s32[1,1,8,12]{3,2,1,0:T(8,128)} %param.16, s32[1,1,8,12]{3,2,1,0:T(8,128)} %param.15, s32[8]{0:T(128)} %bitcast.6), kind=kLoop, calls=%fused_computation.3 | loop fusion | flops 384 | bytes 1184 | tf_op jit(solution)/shard_map/jit(_where)/select_n | solution.py:477
  1.4 0.1 copy.14
  1.5 0.1 select_reduce_fusion
  1.6 0.6 %broadcast_add_fusion.place_ref = s32[8,16]{1,0:T(8,128)} fusion(s32[8,16]{1,0:T(8,128)S(1)} %select_reduce_fusion), kind=kLoop, calls=%fused_computation.5 | loop fusion | flops 128 | bytes 1024 | tf_op jit(solution)/shard_map/add | solution.py:481
  2.2 51.9 %shard_map.128 = (bf16[256,256]{1,0:T(8,128)(2,1)}, bf16[256,256]{1,0:T(8,128)(2,1)}, bf16[2,256,256]{2,1,0:T(8,128)(2,1)}, f32[1,256]{1,0:T(1,128)}) custom-call(s32[8,16]{1,0:T(8,128)} %broadcast_add_fusion.place_ref, bf16[256,256]{1,0:T(8,128)(2,1)} %x_ref.1, bf16[256,256]{1,0:T(8,128)(2,1)} %ws_ref.1, bf16[256,256]{1,0:T(8,128)(2,1)} %wn_ref.1, ...), custom_call_target="tpu_custom_call" | custom-call | flops 2147483648 | bytes 3145728 | tf_op jit(solution)/shard_map/pallas_call | solution.py:486
  54.1 2.0 %shard_map.129 = (bf16[256,256]{1,0:T(8,128)(2,1)}, bf16[256,256]{1,0:T(8,128)(2,1)}, f32[256,256]{1,0:T(8,128)}, f32[256,256]{1,0:T(8,128)}, f32[1,256]{1,0:T(1,128)}) custom-call(bf16[256,256]{1,0:T(8,128)(2,1)} %get-tuple-element.14.a_ref, bf16[256,256]{1,0:T(8,128)(2,1)} %get-tuple-element.15.b_ref, bf16[2,256,256]{2,1,0:T(8,128)(2,1)} %get-tuple-element.16.c_ref, ...), custom_call_target="tpu_custom_call" | custom-call | tf_op jit(solution)/shard_map/pallas_call | solution.py:557
  (2 shorter events, 0.0 us)

commit v3 on v2

--- a/solution.py
+++ b/solution.py
@@ -27,7 +27,9 @@
 
 def kernel(
     cfg,
-    place_ref,
+    counts_ref,
+    trows_ref,
+    tcols_ref,
     x_ref,
     ws_ref,
     wn_ref,
@@ -57,7 +59,10 @@
     gc_buf,
     gc_send,
     ge_buf,
+    place_vec,
+    place_ref,
     vals_sem,
+    place_sem,
     x_rsem,
     x_ssem,
     s1_sems,
@@ -113,6 +118,24 @@
     load = pltpu.make_async_copy(values_ref, vals.at[pl.ds(0, nblk * slots)], vals_sem)
     load.start()
 
+    lanes = place_vec.shape[1]
+    row_at = lax.broadcasted_iota(jnp.int32, (nblk, lanes), 0)
+    lane = lax.broadcasted_iota(jnp.int32, (nblk, lanes), 1)
+
+    def find_places():
+        live = jnp.zeros((nblk, lanes), jnp.int32)
+        for c in range(nblk):
+            live = jnp.where(row_at == c, counts_ref[0, c], live)
+        at = trows_ref[...] * per_dev + tcols_ref[...]
+        found = jnp.full((nblk, lanes), nblk * slots, jnp.int32)
+        for slot in range(slots):
+            hit = jnp.logical_and(at[:, slot : slot + 1] == lane, live > slot)
+            found = jnp.where(hit, row_at * slots + slot, found)
+        place_vec[...] = found
+        move = pltpu.make_async_copy(place_vec, place_ref, place_sem)
+        move.start()
+        return move
+
     barrier = pltpu.get_barrier_semaphore()
     for i in range(1, nblk):
         pl.semaphore_signal(
@@ -146,8 +169,10 @@
         pass_on(x_ref, blk, 0, h, 2, z * 2 + oy, None)
     xg[blk] = x_ref[...]
 
+    move = find_places()
     zself[...] = dot_nn(x_ref[...], ws_ref[...]) + bias_ref[...]
     vals[nblk * slots] = jnp.zeros((tile, tile), BF16)
+    move.wait()
     load.wait()
 
     def place_tiles(c, carry):
@@ -253,12 +278,21 @@
     sig = jax.nn.sigmoid(zvals)
     out_ref[...] = (zvals * sig).astype(BF16)
     dz = (cot_ref[...].astype(F32) * sig * (1.0 + zvals * (1.0 - sig))).astype(BF16)
-    dg[rep] = dot_nt(wn_ref[...], dz).astype(BF16)
-
-    for i in range(chips - 1):
-        to = lax.rem(chip + 1 + i, chips) * 2 + core
-        send(dg.at[rep], dg.at[rep], dg_ssem.at[i], dg_rsem.at[rep], blk, to)
-    send(dg.at[rep], dg.at[rep], dg_ssem.at[chips], dg_rsem.at[rep], blk, mate)
+    fhalf = width // 2
+
+    def pass_dg(q, h, at, to):
+        half_of = dg.at[q, pl.ds(h * fhalf, fhalf)]
+        send(half_of, half_of, dg_ssem.at[at, h], dg_rsem.at[q, h], blk, to)
+
+    def dg_arrived(q, h):
+        arrived(dg.at[q, pl.ds(h * fhalf, fhalf)], dg_ssem.at[0, 0], dg_rsem.at[q, h])
+
+    for h in range(2):
+        at = slice(h * fhalf, (h + 1) * fhalf)
+        dg[rep, at, :] = dot_nt(wn_ref[at, :], dz).astype(BF16)
+        for i in range(chips - 1):
+            pass_dg(rep, h, i, lax.rem(chip + 1 + i, chips) * 2 + core)
+        pass_dg(rep, h, chips, mate)
 
     gown[0] = dot_tn(x_ref[...], dz)
     gown[1] = dot_tn(agg, dz)
@@ -268,6 +302,14 @@
     send(ga_send, ga_recv, ga_sems.at[0], ga_sems.at[1], blk, mate)
     own = dot_nt(dz, ws_ref[...])
     piece = width // nblk
+
+    def pass_chips_dg(h):
+        for i in range(chips - 1):
+            frm = lax.rem(chip + 1 + i, chips) * 2 + core
+            dg_arrived(frm, h)
+            pass_dg(frm, h, chips + 1 + i, mate)
+
+    pass_chips_dg(0)
 
     arrived(ga_recv, ga_sems.at[0], ga_sems.at[1])
     gbias = gbias.astype(BF16).astype(F32) + ga_recv[width : width + PAD, :].astype(F32)
@@ -280,31 +322,25 @@
         to = lax.rem(blk + i, nblk)
         send(gc_send.at[to], gc_buf.at[blk], gc_sems.at[0, to], gc_sems.at[1, blk], to, rep)
 
-    for i in range(chips - 1):
-        frm = lax.rem(chip + 1 + i, chips) * 2 + core
-        arrived(dg.at[frm], dg_ssem.at[0], dg_rsem.at[frm])
-        send(dg.at[frm], dg.at[frm], dg_ssem.at[chips + 1 + i], dg_rsem.at[frm], blk, mate)
-    for i in range(chips):
-        frm = lax.rem(chip + i, chips) * 2 + oc
-        arrived(dg.at[frm], dg_ssem.at[0], dg_rsem.at[frm])
+    pass_chips_dg(1)
 
     for _, copy in pending[before:rep_sends]:
         copy.wait_send()
     del pending[before:rep_sends]
 
-    def term(c):
+    def term(c, lo=0, count=width):
         if nrep <= 4:
-            out = dot_nn(dg[0], dense[c, 0:rows, :])
+            out = dot_nn(dg[0, lo : lo + count], dense[c, 0:rows, :])
             for q in range(1, nrep):
-                out = out + dot_nn(dg[q], dense[c, q * rows : (q + 1) * rows, :])
+                out = out + dot_nn(
+                    dg[q, lo : lo + count], dense[c, q * rows : (q + 1) * rows, :]
+                )
             return out
 
         def step(q, out):
-            return out + dot_nn(dg[q], dense[c, pl.ds(q * rows, rows), :])
-
-        return lax.fori_loop(0, nrep, step, jnp.zeros((width, rows), F32))
-
-    fhalf = width // 2
+            return out + dot_nn(dg[q, lo : lo + count], dense[c, pl.ds(q * rows, rows), :])
+
+        return lax.fori_loop(0, nrep, step, jnp.zeros((count, rows), F32))
 
     def y_copy(dest, h):
         at = pl.ds(h * fhalf, fhalf)
@@ -317,29 +353,7 @@
             device_id_type=MESH,
         )
 
-    near = jnp.minimum(z, nz - 1 - z)
-
-    def send_y(i, carry):
-        dest = jnp.where(
-            i < 2 * near,
-            jnp.where(lax.rem(i, 2) == 0, nz - 1 - i // 2, i // 2),
-            nz - 1 - (i - near),
-        )
-        dest = jnp.where(z < nz // 2, dest, nz - 1 - dest)
-        ysend[dest] = term(dest * 2 + oy).astype(BF16)
-        y_copy(dest, 0).start()
-        y_copy(dest, 1).start()
-        return carry
-
-    lax.fori_loop(0, nz, send_y, 0)
-
-    def own_term(i, carry):
-        acc[pl.ds(i * width, width), :] = term(i * 2 + y)
-        return carry
-
-    lax.fori_loop(0, nz, own_term, 0)
-
-    def grad_sums():
+    def grad_blocks():
         for i in range(1, nblk):
             frm = lax.rem(blk + i, nblk)
             arrived(gc_buf.at[frm], gc_sems.at[0, 0], gc_sems.at[1, frm])
@@ -357,6 +371,8 @@
                 blk,
                 to * 2 + core,
             )
+
+    def grad_chips():
         for i in range(chips - 1):
             frm = lax.rem(chip + 1 + i, chips)
             arrived(gb_buf.at[frm], gb_sems.at[0, 0], gb_sems.at[1, frm])
@@ -370,6 +386,39 @@
             to = lax.rem(blk + i, nblk)
             send(here, here, gd_sems.at[0, to], gd_sems.at[1, blk], to, rep)
 
+    near = jnp.minimum(z, nz - 1 - z)
+
+    def y_dest(i):
+        dest = jnp.where(
+            i < 2 * near,
+            jnp.where(lax.rem(i, 2) == 0, nz - 1 - i // 2, i // 2),
+            nz - 1 - (i - near),
+        )
+        return jnp.where(z < nz // 2, dest, nz - 1 - dest)
+
+    def send_y(i, carry):
+        dest = y_dest(i)
+        ysend[dest] = term(dest * 2 + oy).astype(BF16)
+        y_copy(dest, 0).start()
+        y_copy(dest, 1).start()
+        return carry
+
+    far = y_dest(jnp.int32(0))
+    for h in range(2):
+        for i in range(chips):
+            dg_arrived(lax.rem(chip + i, chips) * 2 + oc, h)
+        at = slice(h * fhalf, (h + 1) * fhalf)
+        ysend[far, at, :] = term(far * 2 + oy, h * fhalf, fhalf).astype(BF16)
+        y_copy(far, h).start()
+    lax.fori_loop(1, nz, send_y, 0)
+    grad_blocks()
+
+    def own_term(i, carry):
+        acc[pl.ds(i * width, width), :] = term(i * 2 + y)
+        return carry
+
+    lax.fori_loop(0, nz, own_term, 0)
+
     def grad_back():
         for i in range(1, nblk):
             frm = lax.rem(blk + i, nblk)
@@ -415,7 +464,7 @@
     at_end = near == 0
     chain(0, 0, z == 0)
     chain(0, 1, z == nz - 1)
-    grad_sums()
+    grad_chips()
     for k in range(nz - 1):
         inside = z >= 0 if k else jnp.logical_not(at_end)
         chain(k, 0, jnp.logical_and(inside, z < nz // 2))
@@ -468,17 +517,9 @@
     nblk, nrep = lax.axis_size("blk"), lax.axis_size("rep")
     slots, tile = tile_values.shape[3], tile_values.shape[4]
     per_dev = rows // tile
-    places = nrep * per_dev * per_dev
+    lanes = max(128, nrep * per_dev * per_dev)
     nz, chips = nblk // 2, nrep // 2
     piece = width // nblk
-
-    slot_place = tile_rows[0, 0] * per_dev + tile_cols[0, 0]
-    slot_ids = lax.broadcasted_iota(jnp.int32, (nblk, slots), 1)
-    slot_place = jnp.where(slot_ids < tile_counts[0, 0][:, None], slot_place, -1)
-    flat = lax.broadcasted_iota(jnp.int32, (nblk, slots), 0) * slots + slot_ids
-    empty = nblk * slots
-    hit = slot_place[:, :, None] == lax.broadcasted_iota(jnp.int32, (1, 1, places), 2)
-    place = empty + jnp.sum(jnp.where(hit, flat[:, :, None] - empty, 0), axis=1)
 
     cfg = (nblk, nrep, slots, tile, rows, width)
     vmem = pl.BlockSpec(memory_space=pltpu.VMEM)
@@ -493,6 +534,8 @@
         ),
         in_specs=[
             pl.BlockSpec(memory_space=pltpu.SMEM),
+            vmem,
+            vmem,
             vmem,
             vmem,
             vmem,
@@ -521,13 +564,16 @@
             pltpu.VMEM((nblk, piece + PAD, width), BF16),
             pltpu.VMEM((nblk, piece + PAD, width), BF16),
             pltpu.VMEM((2, width, width), BF16),
+            pltpu.VMEM((nblk, lanes), jnp.int32),
+            pltpu.SMEM((nblk, lanes), jnp.int32),
+            sems,
             sems,
             sems((nblk, 2)),
             sems((nz, 2, 4)),
             sems((2, chips)),
             sems((2, chips)),
-            sems((nrep,)),
-            sems((2 * chips + 1,)),
+            sems((nrep, 2)),
+            sems((2 * chips + 1, 2)),
             sems((2, nz, 2)),
             sems((nz, 2)),
             sems((2, nz, 2)),
@@ -546,7 +592,9 @@
             transcendentals=rows * width,
         ),
     )(
-        place,
+        tile_counts.reshape(1, nblk),
+        tile_rows.reshape(nblk, slots),
+        tile_cols.reshape(nblk, slots),
         features,
         w_self,
         w_neigh,

time: 57.3 us -> 55.5 us (0.969); the launches traced: 56.1 us -> 55.4 us
  other arithmetic: 1.47 us -> 0 us
  Pallas kernels: 53.9 us -> 54.7 us
    pallas_call x1, Pallas kernels: 51.9 us -> 52.8 us  [local(): pl.pallas_call(functools.partial(kernel, cfg), out_shape=(jax.ShapeDtypeS...]
    select_n x1 -> x0, other arithmetic: 0.78 us -> none  [local(): jnp.where(slot_ids < tile_counts[0, 0][:, None], slot_place, -1)]
    add x1 -> x0, other arithmetic: 0.6 us -> none  [local(): place = empty + jnp.sum(jnp.where(hit, flat[:, :, None] - empty, 0), axis=1)]
where the time goes in v3:
time: 55.5 us; the launch traced here: 55.4 us
  Pallas kernels  54.7 us (99%)
  between operations  0.64 us (1%)
    pallas_call x1, Pallas kernels, local(): pl.pallas_call(functools.partial(kernel, cfg), out_shape=(jax.ShapeDtypeS...  52.8 us
    pallas_call x1, Pallas kernels, local(): pl.pallas_call(hand_out, out_shape=(jax.ShapeDtypeStruct((rows, width), B...  1.98 us

profile of v3, /device:TPU:0, one launch (start us, length us, event | category | flops | bytes accessed | tf_op | source)
XLA Modules:
  0.0 55.4 jit_solution(16921919889452274648)
XLA Ops:
  0.6 52.8 %shard_map.128 = (bf16[256,256]{1,0:T(8,128)(2,1)}, bf16[256,256]{1,0:T(8,128)(2,1)}, bf16[2,256,256]{2,1,0:T(8,128)(2,1)}, f32[1,256]{1,0:T(1,128)}) custom-call(s32[1,8]{1,0:T(1,128)} %bitcast.11, s32[8,12]{1,0:T(8,128)} %bitcast.7, s32[8,12]{1,0:T(8,128)} %bitcast.8, bf16[256,256]{1,0:T(8,128)(2,1)} %x_ref.1, bf16[256,256]{1,0:T(8,128)(2,1)} %ws_ref.1, ...), custom_call_target="tpu_custom_call" | custom-call | flops 2147483648 | bytes 3145728 | tf_op jit(solution)/shard_map/pallas_call | solution.py:527
  53.4 2.0 %shard_map.129 = (bf16[256,256]{1,0:T(8,128)(2,1)}, bf16[256,256]{1,0:T(8,128)(2,1)}, f32[256,256]{1,0:T(8,128)}, f32[256,256]{1,0:T(8,128)}, f32[1,256]{1,0:T(1,128)}) custom-call(bf16[256,256]{1,0:T(8,128)(2,1)} %get-tuple-element.14.a_ref, bf16[256,256]{1,0:T(8,128)(2,1)} %get-tuple-element.15.b_ref, bf16[2,256,256]{2,1,0:T(8,128)(2,1)} %get-tuple-element.16.c_ref, ...), custom_call_target="tpu_custom_call" | custom-call | tf_op jit(solution)/shard_map/pallas_call | solution.py:605

commit v4 on v3

--- a/solution.py
+++ b/solution.py
@@ -147,27 +147,17 @@
         )
     pl.semaphore_wait(barrier, nblk + nrep - 2)
 
-    half = rows // 2
-
-    def pass_on(src, origin, step, h, kind, to_blk, cond):
-        send(
-            src.at[pl.ds(h * half, half)],
-            xg.at[origin, pl.ds(h * half, half)],
-            x_ssem.at[step, h, kind],
-            x_rsem.at[origin, h],
-            to_blk,
-            rep,
-            cond,
-        )
-
-    def half_arrived(origin, h):
-        arrived(xg.at[origin, pl.ds(h * half, half)], x_ssem.at[0, 0, 0], x_rsem.at[origin, h])
+    fhalf = width // 2
+
+    def pass_on(origin, step, h, kind, to_blk, cond):
+        held = xg.at[origin, h]
+        send(held, held, x_ssem.at[step, h, kind], x_rsem.at[origin, h], to_blk, rep, cond)
 
     for h in range(2):
-        pass_on(x_ref, blk, 0, h, 0, blk + 2, z < nz - 1)
-        pass_on(x_ref, blk, 0, h, 1, blk - 2, z > 0)
-        pass_on(x_ref, blk, 0, h, 2, z * 2 + oy, None)
-    xg[blk] = x_ref[...]
+        xg[blk, h] = x_ref[:, h * fhalf : (h + 1) * fhalf]
+        pass_on(blk, 0, h, 0, blk + 2, z < nz - 1)
+        pass_on(blk, 0, h, 1, blk - 2, z > 0)
+        pass_on(blk, 0, h, 2, z * 2 + oy, None)
 
     move = find_places()
     zself[...] = dot_nn(x_ref[...], ws_ref[...]) + bias_ref[...]
@@ -193,14 +183,14 @@
 
     chunk = nrep * rows if nrep <= 4 else rows
 
-    def add_block(c, first=False):
+    def add_block(c, h, first=False):
         def part(i):
             at = pl.ds(i * chunk, chunk)
-            prod = dot_nn(dense[c, at, :], xg[c])
+            prod = dot_nn(dense[c, at, :], xg[c, h])
             if first:
-                acc[at, :] = prod
+                acc[at, h * fhalf : (h + 1) * fhalf] = prod
             else:
-                acc[at, :] += prod
+                acc[at, h * fhalf : (h + 1) * fhalf] += prod
 
         count = nrep * rows // chunk
         if count == 1:
@@ -208,78 +198,126 @@
         else:
             pl.loop(0, count)(part)
 
-    add_block(blk, True)
-
-    def add_pair(step, side, wait):
+    def x_arrived(origin, h):
+        arrived(xg.at[origin, h], x_ssem.at[0, 0, 0], x_rsem.at[origin, h])
+
+    def add_column(step, h):
         for at in (z - step, z + step):
-            origin = at * 2 + side
 
             @pl.when(jnp.logical_and(at >= 0, at < nz))
             def _():
-                if wait:
-                    half_arrived(origin, 0)
-                    half_arrived(origin, 1)
-                add_block(origin)
-
-    for t in range(1, nz):
-        for h in range(2):
-            for at, kind, inner in ((z - t, 0, z < nz - 1), (z + t, 1, z > 0)):
-                origin = at * 2 + y
-                there = at >= 0 if kind == 0 else at < nz
-                on = blk + 2 if kind == 0 else blk - 2
-
-                @pl.when(there)
-                def _():
-                    half_arrived(origin, h)
-
-                held = xg.at[origin]
-                pass_on(held, origin, t, h, kind, on, jnp.logical_and(there, inner))
-                pass_on(held, origin, t, h, kind + 2, z * 2 + oy, there)
-        add_pair(t, y, False)
-        if t == 1:
-            half_arrived(z * 2 + oy, 0)
-            half_arrived(z * 2 + oy, 1)
-            add_block(z * 2 + oy)
-        else:
-            add_pair(t - 1, oy, True)
-    add_pair(nz - 1, oy, True)
+                add_block(at * 2 + y, h)
+
+    def add_across(step, h):
+        for at in (z - step, z + step)[: 2 if step else 1]:
+            origin = at * 2 + oy
+
+            @pl.when(jnp.logical_and(at >= 0, at < nz))
+            def _():
+                x_arrived(origin, h)
+                add_block(origin, h)
+
+    def relay(t, h):
+        for at, kind, inner in ((z - t, 0, z < nz - 1), (z + t, 1, z > 0)):
+            origin = at * 2 + y
+            there = at >= 0 if kind == 0 else at < nz
+            on = blk + 2 if kind == 0 else blk - 2
+
+            @pl.when(there)
+            def _():
+                x_arrived(origin, h)
+
+            pass_on(origin, t, h, kind, on, jnp.logical_and(there, inner))
+            pass_on(origin, t, h, kind + 2, z * 2 + oy, there)
 
     mate = chip * 2 + oc
-    before = len(pending)
-    for i in range(chips):
-        to = lax.rem(chip + 1 + i, chips)
-        zsend[to] = acc[pl.ds((to * 2 + oc) * rows, rows), :].astype(BF16)
-        send(zsend.at[to], s1_recv.at[to], s1_sems.at[0, to], s1_sems.at[1, to], blk, mate)
-    total = None
-    for i in range(chips):
-        to = lax.rem(chip + 1 + i, chips)
-        arrived(s1_recv.at[to], s1_sems.at[0, 0], s1_sems.at[1, to])
-        part = acc[pl.ds((to * 2 + core) * rows, rows), :] + s1_recv[to].astype(F32)
-        if i < chips - 1:
-            ysend[to] = part.astype(BF16)
+    rep_sends = []
+
+    def cores_send(h):
+        cols = pl.ds(h * fhalf, fhalf)
+        start = len(pending)
+        for i in range(chips):
+            to = lax.rem(chip + 1 + i, chips)
+            zsend[to, :, h * fhalf : (h + 1) * fhalf] = acc[
+                pl.ds((to * 2 + oc) * rows, rows), h * fhalf : (h + 1) * fhalf
+            ].astype(BF16)
             send(
-                ysend.at[to],
-                s2_recv.at[chip],
-                s2_sems.at[0, to],
-                s2_sems.at[1, chip],
+                zsend.at[to, :, cols],
+                s1_recv.at[to, :, cols],
+                s1_sems.at[0, to, h],
+                s1_sems.at[1, to, h],
                 blk,
-                to * 2 + core,
+                mate,
             )
-        else:
-            total = part
-    for i in range(chips - 1):
-        frm = lax.rem(chip + 1 + i, chips)
-        arrived(s2_recv.at[frm], s2_sems.at[0, 0], s2_sems.at[1, frm])
-        total = total + s2_recv[frm].astype(F32)
-    agg = total.astype(BF16)
-    rep_sends = len(pending)
-
-    zvals = zself[...] + dot_nn(agg, wn_ref[...])
+        rep_sends.extend(pending[start:])
+        del pending[start:]
+
+    def cores_sum(h):
+        cols = pl.ds(h * fhalf, fhalf)
+        at = slice(h * fhalf, (h + 1) * fhalf)
+        start = len(pending)
+        total = None
+        for i in range(chips):
+            to = lax.rem(chip + 1 + i, chips)
+            arrived(s1_recv.at[to, :, cols], s1_sems.at[0, 0, 0], s1_sems.at[1, to, h])
+            total = acc[pl.ds((to * 2 + core) * rows, rows), at] + s1_recv[to, :, at].astype(F32)
+            if i < chips - 1:
+                ysend[to, :, at] = total.astype(BF16)
+                send(
+                    ysend.at[to, :, cols],
+                    s2_recv.at[chip, :, cols],
+                    s2_sems.at[0, to, h],
+                    s2_sems.at[1, chip, h],
+                    blk,
+                    to * 2 + core,
+                )
+        acc[pl.ds((chip * 2 + core) * rows, rows), at] = total
+        rep_sends.extend(pending[start:])
+        del pending[start:]
+
+    def chips_sum(h):
+        cols = pl.ds(h * fhalf, fhalf)
+        at = slice(h * fhalf, (h + 1) * fhalf)
+        total = acc[pl.ds((chip * 2 + core) * rows, rows), at]
+        for i in range(chips - 1):
+            frm = lax.rem(chip + 1 + i, chips)
+            arrived(s2_recv.at[frm, :, cols], s2_sems.at[0, 0, 0], s2_sems.at[1, frm, h])
+            total = total + s2_recv[frm, :, at].astype(F32)
+        return total.astype(BF16)
+
+    add_block(blk, 0, True)
+    add_block(blk, 1, True)
+    relay(1, 0)
+    relay(1, 1)
+    for t in range(2, nz):
+        add_column(t - 1, 0)
+        relay(t, 0)
+        add_across(t - 2, 0)
+    add_column(nz - 1, 0)
+    for t in range(2, nz):
+        relay(t, 1)
+        add_column(t - 1, 1)
+        if t == 2:
+            add_across(nz - 2, 0)
+    add_across(nz - 1, 0)
+    cores_send(0)
+    add_column(nz - 1, 1)
+    add_across(0, 1)
+    add_across(1, 1)
+    cores_sum(0)
+    for t in range(2, nz):
+        add_across(t, 1)
+    cores_send(1)
+    cores_sum(1)
+    agg0 = chips_sum(0)
+    zpart = zself[...] + dot_nn(agg0, wn_ref[0:fhalf, :])
+    agg1 = chips_sum(1)
+
+    agg = jnp.concatenate([agg0, agg1], axis=1)
+    zvals = zpart + dot_nn(agg1, wn_ref[fhalf:width, :])
     sig = jax.nn.sigmoid(zvals)
     out_ref[...] = (zvals * sig).astype(BF16)
     dz = (cot_ref[...].astype(F32) * sig * (1.0 + zvals * (1.0 - sig))).astype(BF16)
-    fhalf = width // 2
-
     def pass_dg(q, h, at, to):
         half_of = dg.at[q, pl.ds(h * fhalf, fhalf)]
         send(half_of, half_of, dg_ssem.at[at, h], dg_rsem.at[q, h], blk, to)
@@ -324,9 +362,8 @@
 
     pass_chips_dg(1)
 
-    for _, copy in pending[before:rep_sends]:
+    for _, copy in rep_sends:
         copy.wait_send()
-    del pending[before:rep_sends]
 
     def term(c, lo=0, count=width):
         if nrep <= 4:
@@ -547,7 +584,7 @@
         scratch_shapes=[
             pltpu.VMEM((nblk * slots + 1, tile, tile), BF16),
             pltpu.VMEM((nblk, nrep * rows, rows), BF16),
-            pltpu.VMEM((nblk, rows, width), BF16),
+            pltpu.VMEM((nblk, 2, rows, width // 2), BF16),
             pltpu.VMEM((max(nrep * rows, nz * width), width), F32),
             pltpu.VMEM((rows, width), F32),
             pltpu.VMEM((max(chips, nz), rows, width), BF16),
@@ -570,8 +607,8 @@
             sems,
             sems((nblk, 2)),
             sems((nz, 2, 4)),
-            sems((2, chips)),
-            sems((2, chips)),
+            sems((2, chips, 2)),
+            sems((2, chips, 2)),
             sems((nrep, 2)),
             sems((2 * chips + 1, 2)),
             sems((2, nz, 2)),

time: 55.5 us -> 55.5 us (level)
  no operation moved by 1% of the time
where the time goes in v4:
time: 55.5 us; the launch traced here: 55.4 us
  Pallas kernels  54.7 us (99%)
  between operations  0.64 us (1%)
    pallas_call x1, Pallas kernels, local(): pl.pallas_call(functools.partial(kernel, cfg), out_shape=(jax.ShapeDtypeS...  52.7 us
    pallas_call x1, Pallas kernels, local(): pl.pallas_call(hand_out, out_shape=(jax.ShapeDtypeStruct((rows, width), B...  1.98 us

profile of v4, /device:TPU:0, one launch (start us, length us, event | category | flops | bytes accessed | tf_op | source)
XLA Modules:
  0.0 55.4 jit_solution(1942221577109863305)
XLA Ops:
  0.6 52.7 %shard_map.128 = (bf16[256,256]{1,0:T(8,128)(2,1)}, bf16[256,256]{1,0:T(8,128)(2,1)}, bf16[2,256,256]{2,1,0:T(8,128)(2,1)}, f32[1,256]{1,0:T(1,128)}) custom-call(s32[1,8]{1,0:T(1,128)} %bitcast.11, s32[8,12]{1,0:T(8,128)} %bitcast.7, s32[8,12]{1,0:T(8,128)} %bitcast.8, bf16[256,256]{1,0:T(8,128)(2,1)} %x_ref.1, bf16[256,256]{1,0:T(8,128)(2,1)} %ws_ref.1, ...), custom_call_target="tpu_custom_call" | custom-call | flops 2147483648 | bytes 3145728 | tf_op jit(solution)/shard_map/pallas_call | solution.py:564
  53.4 2.0 %shard_map.129 = (bf16[256,256]{1,0:T(8,128)(2,1)}, bf16[256,256]{1,0:T(8,128)(2,1)}, f32[256,256]{1,0:T(8,128)}, f32[256,256]{1,0:T(8,128)}, f32[1,256]{1,0:T(1,128)}) custom-call(bf16[256,256]{1,0:T(8,128)(2,1)} %get-tuple-element.14.a_ref, bf16[256,256]{1,0:T(8,128)(2,1)} %get-tuple-element.15.b_ref, bf16[2,256,256]{2,1,0:T(8,128)(2,1)} %get-tuple-element.16.c_ref, ...), custom_call_target="tpu_custom_call" | custom-call | tf_op jit(solution)/shard_map/pallas_call | solution.py:642

commit v5 on v3

--- a/solution.py
+++ b/solution.py
@@ -149,24 +149,25 @@
 
     half = rows // 2
 
-    def pass_on(src, origin, step, h, kind, to_blk, cond):
-        send(
-            src.at[pl.ds(h * half, half)],
-            xg.at[origin, pl.ds(h * half, half)],
-            x_ssem.at[step, h, kind],
-            x_rsem.at[origin, h],
-            to_blk,
-            rep,
-            cond,
+    def relay_copy(src, origin, step, h, kind):
+        to = (blk + 2, blk - 2, z * 2 + oy, z * 2 + oy)[kind]
+        return pltpu.make_async_remote_copy(
+            src_ref=src.at[pl.ds(h * half, half)],
+            dst_ref=xg.at[origin, pl.ds(h * half, half)],
+            send_sem=x_ssem.at[step, h, kind],
+            recv_sem=x_rsem.at[origin, h],
+            device_id=(to, rep),
+            device_id_type=MESH,
         )
 
     def half_arrived(origin, h):
         arrived(xg.at[origin, pl.ds(h * half, half)], x_ssem.at[0, 0, 0], x_rsem.at[origin, h])
 
+    inner = (z < nz - 1, z > 0)
     for h in range(2):
-        pass_on(x_ref, blk, 0, h, 0, blk + 2, z < nz - 1)
-        pass_on(x_ref, blk, 0, h, 1, blk - 2, z > 0)
-        pass_on(x_ref, blk, 0, h, 2, z * 2 + oy, None)
+        pl.when(inner[0])(relay_copy(x_ref, blk, 0, h, 0).start)
+        pl.when(inner[1])(relay_copy(x_ref, blk, 0, h, 1).start)
+        relay_copy(x_ref, blk, 0, h, 2).start()
     xg[blk] = x_ref[...]
 
     move = find_places()
@@ -193,14 +194,10 @@
 
     chunk = nrep * rows if nrep <= 4 else rows
 
-    def add_block(c, first=False):
+    def add_block(c):
         def part(i):
             at = pl.ds(i * chunk, chunk)
-            prod = dot_nn(dense[c, at, :], xg[c])
-            if first:
-                acc[at, :] = prod
-            else:
-                acc[at, :] += prod
+            acc[at, :] += dot_nn(dense[c, at, :], xg[c])
 
         count = nrep * rows // chunk
         if count == 1:
@@ -208,41 +205,44 @@
         else:
             pl.loop(0, count)(part)
 
-    add_block(blk, True)
-
-    def add_pair(step, side, wait):
-        for at in (z - step, z + step):
-            origin = at * 2 + side
-
-            @pl.when(jnp.logical_and(at >= 0, at < nz))
-            def _():
-                if wait:
-                    half_arrived(origin, 0)
-                    half_arrived(origin, 1)
-                add_block(origin)
-
-    for t in range(1, nz):
+    acc[...] = jnp.zeros_like(acc)
+
+    def gather_step(t, carry):
         for h in range(2):
-            for at, kind, inner in ((z - t, 0, z < nz - 1), (z + t, 1, z > 0)):
-                origin = at * 2 + y
-                there = at >= 0 if kind == 0 else at < nz
-                on = blk + 2 if kind == 0 else blk - 2
+            for way in range(2):
+                at = z - t if way == 0 else z + t
+                there = jnp.logical_and(jnp.logical_and(at >= 0, at < nz), t > 0)
+                origin = jnp.clip(at, 0, nz - 1) * 2 + y
 
                 @pl.when(there)
                 def _():
                     half_arrived(origin, h)
-
-                held = xg.at[origin]
-                pass_on(held, origin, t, h, kind, on, jnp.logical_and(there, inner))
-                pass_on(held, origin, t, h, kind + 2, z * 2 + oy, there)
-        add_pair(t, y, False)
-        if t == 1:
-            half_arrived(z * 2 + oy, 0)
-            half_arrived(z * 2 + oy, 1)
-            add_block(z * 2 + oy)
-        else:
-            add_pair(t - 1, oy, True)
-    add_pair(nz - 1, oy, True)
+                    relay_copy(xg.at[origin], origin, t, h, way + 2).start()
+                    pl.when(inner[way])(relay_copy(xg.at[origin], origin, t, h, way).start)
+
+        def add_one(k, carry):
+            across = k // 2
+            away = t - across
+            at = jnp.where(lax.rem(k, 2) == 0, z - away, z + away)
+            there = jnp.logical_and(at >= 0, at < nz)
+            there = jnp.logical_and(there, jnp.logical_and(away >= 0, away < nz))
+            there = jnp.logical_and(there, jnp.logical_or(away > 0, lax.rem(k, 2) == 0))
+            origin = jnp.clip(at, 0, nz - 1) * 2 + jnp.where(across == 0, y, oy)
+
+            @pl.when(there)
+            def _():
+                @pl.when(across == 1)
+                def _():
+                    half_arrived(origin, 0)
+                    half_arrived(origin, 1)
+
+                add_block(origin)
+
+            return carry
+
+        return lax.fori_loop(0, 4, add_one, carry)
+
+    lax.fori_loop(0, nz + 1, gather_step, 0)
 
     mate = chip * 2 + oc
     before = len(pending)
@@ -403,14 +403,10 @@
         y_copy(dest, 1).start()
         return carry
 
-    far = y_dest(jnp.int32(0))
     for h in range(2):
         for i in range(chips):
             dg_arrived(lax.rem(chip + i, chips) * 2 + oc, h)
-        at = slice(h * fhalf, (h + 1) * fhalf)
-        ysend[far, at, :] = term(far * 2 + oy, h * fhalf, fhalf).astype(BF16)
-        y_copy(far, h).start()
-    lax.fori_loop(1, nz, send_y, 0)
+    lax.fori_loop(0, nz, send_y, 0)
     grad_blocks()
 
     def own_term(i, carry):
@@ -432,15 +428,32 @@
         arrived(buf.at[pl.ds(h * fhalf, fhalf)], z_ssem.at[0, 0], sem)
         acc[at, :] += buf[h * fhalf : (h + 1) * fhalf, :].astype(F32)
 
-    def chain(k, way, cond):
-        dest = nz - 1 - k if way == 0 else k
-        on = blk + 2 if way == 0 else blk - 2
-        more = z > 0 if way == 0 else z < nz - 1
-        cond = jnp.logical_and(cond, z < dest if way == 0 else z > dest)
-        for h in range(2):
-
-            @pl.when(cond)
-            def _():
+    def chain_at(j):
+        way = jnp.where(z < nz // 2, lax.rem(j, 2), 1 - lax.rem(j, 2))
+        dest = jnp.where(way == 0, nz - 1 - j // 2, j // 2)
+        on = jnp.where(way == 0, blk + 2, blk - 2)
+        cond = jnp.where(way == 0, z < dest, z > dest)
+        more = jnp.where(way == 0, z > 0, z < nz - 1)
+
+        def copy(h):
+            at = pl.ds(h * fhalf, fhalf)
+            return pltpu.make_async_remote_copy(
+                src_ref=zsend.at[dest, at],
+                dst_ref=zrecv.at[way, dest, at],
+                send_sem=z_ssem.at[dest, h],
+                recv_sem=z_rsem.at[way, dest, h],
+                device_id=(on, rep),
+                device_id_type=MESH,
+            )
+
+        return way, dest, cond, more, copy
+
+    def chain(j, carry):
+        way, dest, cond, more, copy = chain_at(j)
+
+        @pl.when(cond)
+        def _():
+            for h in range(2):
                 add_from(yrecv.at[dest], dest, h, y_sems.at[1, dest, h])
 
                 @pl.when(more)
@@ -449,27 +462,12 @@
 
                 rows_at = pl.ds(dest * width + h * fhalf, fhalf)
                 zsend[dest, h * fhalf : (h + 1) * fhalf, :] = acc[rows_at, :].astype(BF16)
-
-            at = pl.ds(h * fhalf, fhalf)
-            send(
-                zsend.at[dest, at],
-                zrecv.at[way, dest, at],
-                z_ssem.at[dest, h],
-                z_rsem.at[way, dest, h],
-                on,
-                rep,
-                cond,
-            )
-
-    at_end = near == 0
-    chain(0, 0, z == 0)
-    chain(0, 1, z == nz - 1)
+                copy(h).start()
+
+        return carry
+
     grad_chips()
-    for k in range(nz - 1):
-        inside = z >= 0 if k else jnp.logical_not(at_end)
-        chain(k, 0, jnp.logical_and(inside, z < nz // 2))
-        chain(k, 1, inside)
-        chain(k, 0, jnp.logical_and(inside, z >= nz // 2))
+    lax.fori_loop(0, 2 * (nz - 1), chain, 0)
 
     grad_back()
     for h in range(2):
@@ -500,6 +498,35 @@
         return carry
 
     lax.fori_loop(0, nz, drain_y, 0)
+
+    def drain_chain(j, carry):
+        _, _, cond, _, copy = chain_at(j)
+
+        @pl.when(cond)
+        def _():
+            copy(0).wait_send()
+            copy(1).wait_send()
+
+        return carry
+
+    lax.fori_loop(0, 2 * (nz - 1), drain_chain, 0)
+
+    def drain_relay(t, carry):
+        for way in range(2):
+            at = z - t if way == 0 else z + t
+            there = jnp.logical_and(at >= 0, at < nz)
+            origin = jnp.clip(at, 0, nz - 1) * 2 + y
+            for h in range(2):
+                onward = relay_copy(xg.at[origin], origin, t, h, way)
+                pl.when(jnp.logical_and(there, inner[way]))(onward.wait_send)
+                over = relay_copy(xg.at[origin], origin, t, h, way + 2)
+                if way == 0:
+                    pl.when(there)(over.wait_send)
+                else:
+                    pl.when(jnp.logical_and(there, t > 0))(over.wait_send)
+        return carry
+
+    lax.fori_loop(0, nz, drain_relay, 0)
 
 
 def hand_out(a_ref, b_ref, c_ref, d_ref, out_ref, gradf_ref, gs_ref, gn_ref, gb_ref):

time: 55.5 us -> 58.4 us (1.052)
  Pallas kernels: 54.7 us -> 57.6 us
    pallas_call x1, Pallas kernels: 52.8 us -> 55.6 us  [local(): pl.pallas_call(functools.partial(kernel, cfg), out_shape=(jax.ShapeDtypeS...]
where the time goes in v5:
time: 58.4 us; the launch traced here: 58.2 us
  Pallas kernels  57.6 us (99%)
  between operations  0.64 us (1%)
    pallas_call x1, Pallas kernels, local(): pl.pallas_call(functools.partial(kernel, cfg), out_shape=(jax.ShapeDtypeS...  55.6 us
    pallas_call x1, Pallas kernels, local(): pl.pallas_call(hand_out, out_shape=(jax.ShapeDtypeStruct((rows, width), B...  1.98 us

profile of v5, /device:TPU:0, one launch (start us, length us, event | category | flops | bytes accessed | tf_op | source)
XLA Modules:
  0.0 58.2 jit_solution(9753404999546115279)
XLA Ops:
  0.6 55.6 %shard_map.128 = (bf16[256,256]{1,0:T(8,128)(2,1)}, bf16[256,256]{1,0:T(8,128)(2,1)}, bf16[2,256,256]{2,1,0:T(8,128)(2,1)}, f32[1,256]{1,0:T(1,128)}) custom-call(s32[1,8]{1,0:T(1,128)} %bitcast.11, s32[8,12]{1,0:T(8,128)} %bitcast.7, s32[8,12]{1,0:T(8,128)} %bitcast.8, bf16[256,256]{1,0:T(8,128)(2,1)} %x_ref.1, bf16[256,256]{1,0:T(8,128)(2,1)} %ws_ref.1, ...), custom_call_target="tpu_custom_call" | custom-call | flops 2147483648 | bytes 3145728 | tf_op jit(solution)/shard_map/pallas_call | solution.py:554
  56.3 2.0 %shard_map.129 = (bf16[256,256]{1,0:T(8,128)(2,1)}, bf16[256,256]{1,0:T(8,128)(2,1)}, f32[256,256]{1,0:T(8,128)}, f32[256,256]{1,0:T(8,128)}, f32[1,256]{1,0:T(1,128)}) custom-call(bf16[256,256]{1,0:T(8,128)(2,1)} %get-tuple-element.14.a_ref, bf16[256,256]{1,0:T(8,128)(2,1)} %get-tuple-element.15.b_ref, bf16[2,256,256]{2,1,0:T(8,128)(2,1)} %get-tuple-element.16.c_ref, ...), custom_call_target="tpu_custom_call" | custom-call | tf_op jit(solution)/shard_map/pallas_call | solution.py:632

commit v6 on v3

--- a/solution.py
+++ b/solution.py
@@ -147,12 +147,12 @@
         )
     pl.semaphore_wait(barrier, nblk + nrep - 2)
 
-    half = rows // 2
+    part = rows // 4
 
     def pass_on(src, origin, step, h, kind, to_blk, cond):
         send(
-            src.at[pl.ds(h * half, half)],
-            xg.at[origin, pl.ds(h * half, half)],
+            src.at[pl.ds(h * part, part)],
+            xg.at[origin, pl.ds(h * part, part)],
             x_ssem.at[step, h, kind],
             x_rsem.at[origin, h],
             to_blk,
@@ -160,10 +160,10 @@
             cond,
         )
 
-    def half_arrived(origin, h):
-        arrived(xg.at[origin, pl.ds(h * half, half)], x_ssem.at[0, 0, 0], x_rsem.at[origin, h])
-
-    for h in range(2):
+    def part_arrived(origin, h):
+        arrived(xg.at[origin, pl.ds(h * part, part)], x_ssem.at[0, 0, 0], x_rsem.at[origin, h])
+
+    for h in range(4):
         pass_on(x_ref, blk, 0, h, 0, blk + 2, z < nz - 1)
         pass_on(x_ref, blk, 0, h, 1, blk - 2, z > 0)
         pass_on(x_ref, blk, 0, h, 2, z * 2 + oy, None)
@@ -217,12 +217,12 @@
             @pl.when(jnp.logical_and(at >= 0, at < nz))
             def _():
                 if wait:
-                    half_arrived(origin, 0)
-                    half_arrived(origin, 1)
+                    for h in range(4):
+                        part_arrived(origin, h)
                 add_block(origin)
 
     for t in range(1, nz):
-        for h in range(2):
+        for h in range(4):
             for at, kind, inner in ((z - t, 0, z < nz - 1), (z + t, 1, z > 0)):
                 origin = at * 2 + y
                 there = at >= 0 if kind == 0 else at < nz
@@ -230,15 +230,15 @@
 
                 @pl.when(there)
                 def _():
-                    half_arrived(origin, h)
+                    part_arrived(origin, h)
 
                 held = xg.at[origin]
                 pass_on(held, origin, t, h, kind, on, jnp.logical_and(there, inner))
                 pass_on(held, origin, t, h, kind + 2, z * 2 + oy, there)
         add_pair(t, y, False)
         if t == 1:
-            half_arrived(z * 2 + oy, 0)
-            half_arrived(z * 2 + oy, 1)
+            for h in range(4):
+                part_arrived(z * 2 + oy, h)
             add_block(z * 2 + oy)
         else:
             add_pair(t - 1, oy, True)
@@ -568,8 +568,8 @@
             pltpu.SMEM((nblk, lanes), jnp.int32),
             sems,
             sems,
-            sems((nblk, 2)),
-            sems((nz, 2, 4)),
+            sems((nblk, 4)),
+            sems((nz, 4, 4)),
             sems((2, chips)),
             sems((2, chips)),
             sems((nrep, 2)),

time: 55.5 us -> 54.4 us (0.980)
  Pallas kernels: 54.7 us -> 53.6 us
    pallas_call x1, Pallas kernels: 52.8 us -> 51.6 us  [local(): pl.pallas_call(functools.partial(kernel, cfg), out_shape=(jax.ShapeDtypeS...]
where the time goes in v6:
time: 54.4 us; the launch traced here: 54.2 us
  Pallas kernels  53.6 us (99%)
  between operations  0.64 us (1%)
    pallas_call x1, Pallas kernels, local(): pl.pallas_call(functools.partial(kernel, cfg), out_shape=(jax.ShapeDtypeS...  51.6 us
    pallas_call x1, Pallas kernels, local(): pl.pallas_call(hand_out, out_shape=(jax.ShapeDtypeStruct((rows, width), B...  1.98 us

profile of v6, /device:TPU:0, one launch (start us, length us, event | category | flops | bytes accessed | tf_op | source)
XLA Modules:
  0.0 54.2 jit_solution(5093461072742952625)
XLA Ops:
  0.6 51.6 %shard_map.128 = (bf16[256,256]{1,0:T(8,128)(2,1)}, bf16[256,256]{1,0:T(8,128)(2,1)}, bf16[2,256,256]{2,1,0:T(8,128)(2,1)}, f32[1,256]{1,0:T(1,128)}) custom-call(s32[1,8]{1,0:T(1,128)} %bitcast.11, s32[8,12]{1,0:T(8,128)} %bitcast.7, s32[8,12]{1,0:T(8,128)} %bitcast.8, bf16[256,256]{1,0:T(8,128)(2,1)} %x_ref.1, bf16[256,256]{1,0:T(8,128)(2,1)} %ws_ref.1, ...), custom_call_target="tpu_custom_call" | custom-call | flops 2147483648 | bytes 3145728 | tf_op jit(solution)/shard_map/pallas_call | solution.py:527
  52.2 2.0 %shard_map.129 = (bf16[256,256]{1,0:T(8,128)(2,1)}, bf16[256,256]{1,0:T(8,128)(2,1)}, f32[256,256]{1,0:T(8,128)}, f32[256,256]{1,0:T(8,128)}, f32[1,256]{1,0:T(1,128)}) custom-call(bf16[256,256]{1,0:T(8,128)(2,1)} %get-tuple-element.14.a_ref, bf16[256,256]{1,0:T(8,128)(2,1)} %get-tuple-element.15.b_ref, bf16[2,256,256]{2,1,0:T(8,128)(2,1)} %get-tuple-element.16.c_ref, ...), custom_call_target="tpu_custom_call" | custom-call | tf_op jit(solution)/shard_map/pallas_call | solution.py:605
